TPU v7x, 32 devices: a whole 2x2x4 slice. The times are simulated.
32 devices in a mesh: rep: 4 (over x, core), shard: 8 (over z, y).
Axes of the slice: x: 2, y: 2, z: 4, core: 2. Of those that a mesh axis runs over, the one named last changes fastest.
Arguments:
- tokens: bfloat16 [16384, 768], P(('rep', 'shard')), may hold values from -6 to 6
- w_qkv: bfloat16 [768, 2304], P('shard'), may hold values from -0.21875 to 0.21875
- w_out: bfloat16 [768, 768], P('shard'), may hold values from -1.75 to 1.75
- w_up: bfloat16 [768, 3072], P('shard'), may hold values from -0.21875 to 0.21875
- w_down: bfloat16 [3072, 768], P('shard'), may hold values from -0.109375 to 0.109375
- gain_attn: bfloat16 [768], P('shard'), may hold values from 0.099609375 to 1.8984375
- gain_mlp: bfloat16 [768], P('shard'), may hold values from 0.099609375 to 1.8984375
- d_out: bfloat16 [16384, 768], P(('rep', 'shard')), may hold values from -6 to 6
Outputs:
- block_out: bfloat16 [16384, 768], P(('rep', 'shard'))
- d_tokens: float32 [16384, 768], P(('rep', 'shard'))
- d_w_qkv: float32 [768, 2304], P('shard')
- d_w_out: float32 [768, 768], P('shard')
- d_w_up: float32 [768, 3072], P('shard')
- d_w_down: float32 [3072, 768], P('shard')
- d_gain_attn: float32 [768], P('shard')
- d_gain_mlp: float32 [768], P('shard')
All inputs are finite; a program needn't handle non-finite values.
Results may differ from a plain program's by a relative error of at most 0.015.
Values may be sent and summed in bfloat16 or wider, within the bound.
No kernel may reach another device: no remote copies, remote signals or barrier semaphores. Data moves between devices by JAX's collectives and lax.ppermute only.
A program may use at most 256 MiB of HBM per device.

v0:
```python
import jax
import jax.numpy as jnp
from jax import lax
from jax.experimental import pallas as pl
from jax.experimental.pallas import tpu as pltpu
from jax.sharding import PartitionSpec as P

D = 768
HEADS = 12
HDIM = 64
FF = 3072
PR = 128
PLEN = 1024
KEYS = PLEN + 2 * PR
ROWS = 4 * PR
PAIRS = HEADS // 2
WIDTH = 2 * HDIM
HALF = 1536
WIDE = HALF + 128
SUB = 48
LEFT = 896
RIGHT = D + 128
UNIT = 2 * PR
FSUB = 96
FH = FF // 2
norm_eps = 1e-05
neg_fill = -1e30
SCALE = HDIM ** (-0.5)
GELU_C = 0.7978845608028654
GELU_A = 0.044715
BF = jnp.bfloat16
F32 = jnp.float32
VMEM_LIMIT = 60 * 1024 * 1024
BLOCKS = (0, 1, 2, 3, 4, 5, 6, 7)
ORDER = (0, 2, 4, 6, 1, 3, 5, 7)


def dot_nt(a, b):
    return lax.dot_general(a, b, (((1,), (1,)), ((), ())), preferred_element_type=F32)


def dot_tn(a, b):
    return lax.dot_general(a, b, (((0,), (0,)), ((), ())), preferred_element_type=F32)


def dot_nn(a, b):
    return jnp.dot(a, b, preferred_element_type=F32)


def rms_inv(values):
    return lax.rsqrt(jnp.mean(values * values, axis=-1, keepdims=True) + norm_eps)


def params():
    return pltpu.CompilerParams(vmem_limit_bytes=VMEM_LIMIT)


def shape(dims, dtype):
    return jax.ShapeDtypeStruct(dims, dtype)


def fill_normed(x_ref, gain, normed_ref):
    @pl.loop(0, KEYS, step=PR)
    def _(row):
        rows = pl.ds(pl.multiple_of(row, PR), PR)
        part = x_ref[rows, :].astype(F32)
        normed_ref[rows, :] = (part * rms_inv(part) * gain).astype(BF)


def lane_half(head):
    lanes = lax.broadcasted_iota(jnp.int32, (1, WIDTH), 1)
    return (lanes >= HDIM) if head else (lanes < HDIM)


def gain_row(column):
    return column.astype(F32).T[0:1, :]


def attn_fwd_kernel(
    where_ref, x_ref, l00_ref, l10_ref, l01_ref, l11_ref, r00_ref, r10_ref, r01_ref, r11_ref,
    w_ref, q_ref, k_ref, v_ref, e_ref, ec_ref, o_ref, r_ref, mid_ref, nm_ref, normed_ref,
    bias_ref, att_ref, qs_ref, s_ref, inv_ref, out_ref, sems,
):
    step = pl.program_id(0)

    @pl.when(step == 0)
    def _():
        side, core = where_ref[1], where_ref[2]
        copies = []
        for at, (dx, dc, piece) in enumerate(
            ((0, 0, l00_ref), (1, 0, l10_ref), (0, 1, l01_ref), (1, 1, l11_ref))
        ):
            for i in range(8):
                start = where_ref[8 + i] * (2 * SUB) + jnp.bitwise_xor(side, dx) * SUB
                copies.append(
                    pltpu.make_async_copy(
                        piece.at[i],
                        w_ref.at[
                            jnp.bitwise_xor(core, dc),
                            pl.ds(pl.multiple_of(start, 16), SUB),
                            pl.ds(0, LEFT),
                        ],
                        sems.at[at * 8 + i],
                    )
                )
        for at, (far, dc, piece) in enumerate(
            ((0, 0, r00_ref), (1, 0, r10_ref), (0, 1, r01_ref), (1, 1, r11_ref))
        ):
            for i in range(8):
                start = where_ref[8 + far * 4 + i % 4] * (2 * SUB)
                start = start + jnp.bitwise_xor(side, i // 4) * SUB
                copies.append(
                    pltpu.make_async_copy(
                        piece.at[i],
                        w_ref.at[
                            jnp.bitwise_xor(core, dc),
                            pl.ds(pl.multiple_of(start, 16), SUB),
                            pl.ds(LEFT, WIDE - LEFT),
                        ],
                        sems.at[32 + at * 8 + i],
                    )
                )
        for copy in copies:
            copy.start()
        pos = where_ref[0]
        row = lax.broadcasted_iota(jnp.int32, (PR, PR), 0)
        col = lax.broadcasted_iota(jnp.int32, (PR, PR), 1)
        tri = jnp.where(col <= row, 0.0, neg_fill)
        for part in range(2):
            mine = jnp.bitwise_xor(pos, BLOCKS[part])
            for block in range(8):
                at = (pl.ds(part * PR, PR), pl.ds(block * PR, PR))
                if block == part:
                    bias_ref[at] = tri
                else:
                    seen = jnp.bitwise_xor(pos, BLOCKS[block]) < mine
                    bias_ref[at] = jnp.full((PR, PR), jnp.where(seen, 0.0, neg_fill), F32)
        for copy in copies:
            copy.wait()
        fill_normed(x_ref, gain_row(w_ref[0, :, HALF:]), normed_ref)

    at = pl.ds(pl.multiple_of(step * UNIT, UNIT), UNIT)
    at_k = pl.ds(pl.multiple_of(D + step * UNIT, UNIT), UNIT)
    k_ref[...] = dot_nn(normed_ref[...], w_ref[0, :, at_k]).astype(BF)
    v_ref[...] = dot_nn(normed_ref[...], w_ref[1, :, at]).astype(BF)
    wq = w_ref[0, :, at]
    q_ref[0:UNIT, :] = (dot_nn(normed_ref[0:UNIT, :], wq) * SCALE).astype(BF)
    q_ref[UNIT:, :] = (dot_nn(normed_ref[PLEN:, :], wq) * SCALE).astype(BF)
    row = lax.broadcasted_iota(jnp.int32, (PR, PR), 0)
    col = lax.broadcasted_iota(jnp.int32, (PR, PR), 1)
    tri = jnp.where(col <= row, 0.0, neg_fill)
    low_half = lane_half(0)
    for pair in range(2):
        lanes = slice(pair * WIDTH, (pair + 1) * WIDTH)
        query = q_ref[:, lanes]
        for head in range(2):
            rows = slice(head * ROWS, (head + 1) * ROWS)
            qs_ref[rows, :] = jnp.where(lane_half(head), query, jnp.zeros_like(query))
        s_ref[...] = dot_nt(qs_ref[...], k_ref[0:PLEN, lanes])
        for head in range(2):
            for chunk in range(4):
                mine = slice(chunk * PR, (chunk + 1) * PR)
                rows = slice(head * ROWS + chunk * PR, head * ROWS + (chunk + 1) * PR)
                scores = s_ref[rows, :]
                if chunk < 2:
                    scores = scores + bias_ref[mine, :]
                    top = jnp.max(scores, axis=-1, keepdims=True)
                    terms = jnp.exp(scores - top)
                    total = jnp.sum(terms, axis=-1, keepdims=True)
                else:
                    own = slice(PLEN + (chunk - 2) * PR, PLEN + (chunk - 1) * PR)
                    near = dot_nt(qs_ref[rows, :], k_ref[own, lanes]) + tri
                    top = jnp.maximum(
                        jnp.max(scores, axis=-1, keepdims=True),
                        jnp.max(near, axis=-1, keepdims=True),
                    )
                    terms = jnp.exp(scores - top)
                    near_terms = jnp.exp(near - top)
                    total = jnp.sum(terms, axis=-1, keepdims=True) + jnp.sum(
                        near_terms, axis=-1, keepdims=True
                    )
                    ec_ref[2 * pair + head, (chunk - 2) * PR : (chunk - 1) * PR, :] = (
                        near_terms.astype(BF)
                    )
                e_ref[2 * pair + head, mine, :] = terms.astype(BF)
                inv_ref[rows, :] = jnp.broadcast_to(1.0 / total, (PR, WIDTH))
        terms = e_ref[2 * pair : 2 * pair + 2].reshape(2 * ROWS, PLEN)
        out_ref[...] = dot_nn(terms, v_ref[0:PLEN, lanes])
        for head in range(2):
            for side in range(2):
                own = slice(PLEN + side * PR, PLEN + (side + 1) * PR)
                start = head * ROWS + (2 + side) * PR
                near = ec_ref[2 * pair + head, side * PR : (side + 1) * PR, :]
                out_ref[start : start + PR, :] += dot_nn(near, v_ref[own, lanes])
        inv = jnp.where(low_half, inv_ref[0:ROWS, :], inv_ref[ROWS:, :])
        r_ref[:, lanes] = inv
        o_ref[:, lanes] = (
            jnp.where(low_half, out_ref[0:ROWS, :], out_ref[ROWS:, :]) * inv
        ).astype(BF)
    att_ref[step] = o_ref[...]

    @pl.when(step == pl.num_programs(0) - 1)
    def _():
        wout = w_ref[1, :, D:HALF]
        gain = gain_row(w_ref[1, :, HALF:])
        for chunk in range(4):
            rows = slice(chunk * PR, (chunk + 1) * PR)
            from_row = chunk * PR if chunk < 2 else PLEN + (chunk - 2) * PR
            middle = x_ref[from_row : from_row + PR, :].astype(F32)
            for i in range(3):
                middle = middle + dot_nn(att_ref[i, rows, :], wout[i * UNIT : (i + 1) * UNIT, :])
            mid_ref[rows, :] = middle
            nm_ref[rows, :] = (middle * rms_inv(middle) * gain).astype(BF)


def attn_fwd(where, x_all, pieces):
    pair = lambda i: (0, i)
    whole = lambda i: (0, 0)
    heads = lambda i: (i, 0, 0)
    anywhere = pl.BlockSpec(memory_space=pl.ANY)
    return pl.pallas_call(
        attn_fwd_kernel,
        grid=(3,),
        in_specs=[
            pl.BlockSpec(memory_space=pltpu.SMEM),
            pl.BlockSpec((KEYS, D), whole),
            *[anywhere] * 8,
        ],
        out_specs=[
            pl.BlockSpec((2, D, WIDE), lambda i: (0, 0, 0)),
            pl.BlockSpec((ROWS, UNIT), pair),
            pl.BlockSpec((KEYS, UNIT), pair),
            pl.BlockSpec((KEYS, UNIT), pair),
            pl.BlockSpec((4, ROWS, PLEN), heads),
            pl.BlockSpec((4, UNIT, PR), heads),
            pl.BlockSpec((ROWS, UNIT), pair),
            pl.BlockSpec((ROWS, UNIT), pair),
            pl.BlockSpec((ROWS, D), whole),
            pl.BlockSpec((ROWS, D), whole),
            pl.BlockSpec((KEYS, D), whole),
        ],
        out_shape=[
            shape((2, D, WIDE), BF),
            shape((ROWS, D), BF),
            shape((KEYS, D), BF),
            shape((KEYS, D), BF),
            shape((HEADS, ROWS, PLEN), BF),
            shape((HEADS, 2 * PR, PR), BF),
            shape((ROWS, D), BF),
            shape((ROWS, D), F32),
            shape((ROWS, D), F32),
            shape((ROWS, D), BF),
            shape((KEYS, D), BF),
        ],
        scratch_shapes=[
            pltpu.VMEM((2 * PR, PLEN), F32),
            pltpu.VMEM((3, ROWS, UNIT), BF),
            pltpu.VMEM((2 * ROWS, WIDTH), BF),
            pltpu.VMEM((2 * ROWS, PLEN), F32),
            pltpu.VMEM((2 * ROWS, WIDTH), F32),
            pltpu.VMEM((2 * ROWS, WIDTH), F32),
            pltpu.SemaphoreType.DMA((64,)),
        ],
        compiler_params=params(),
        cost_estimate=pl.CostEstimate(
            flops=30_000_000_000, bytes_accessed=30_000_000, transcendentals=6_300_000
        ),
    )(where, x_all, *pieces)


def mlp_kernel(
    where_ref, nm0_ref, nm1_ref, g0_ref, g1_ref,
    up00_ref, up10_ref, up01_ref, up11_ref, down00_ref, down10_ref, down01_ref, down11_ref,
    e_ref, y_ref, give_e_ref, give_y_ref, up_keep_ref, up_give_ref, down_keep_ref, down_give_ref,
    wup_ref, wdown_ref, nm_ref, g_ref, acc_e_ref, acc_y_ref, part_ref, active_ref, d_hidden_ref, sems,
):
    step = pl.program_id(0)
    side, y_at = where_ref[1], where_ref[0] % 2

    @pl.when(step == 0)
    def _():
        copies = []
        for dy, ups, downs in (
            (0, (up00_ref, up10_ref), (down00_ref, down10_ref)),
            (1, (up01_ref, up11_ref), (down01_ref, down11_ref)),
        ):
            for dx in range(2):
                for i in range(4):
                    block = where_ref[8 + dy * 4 + i] * 2 + jnp.bitwise_xor(side, dx)
                    rows = pl.ds(pl.multiple_of(block * SUB, 16), SUB)
                    for half in range(2):
                        copies.append(
                            pltpu.make_async_copy(
                                ups[dx].at[i, pl.ds(half * SUB, SUB), :],
                                wup_ref.at[rows, pl.ds(half * D, D)],
                                sems.at[len(copies)],
                            )
                        )
                    copies.append(
                        pltpu.make_async_copy(
                            downs[dx].at[i],
                            wdown_ref.at[pl.ds(pl.multiple_of(block * FSUB, 16), FSUB), :],
                            sems.at[len(copies)],
                        )
                    )
        for copy in copies:
            copy.start()
        nm_ref[0:ROWS, :] = nm0_ref[...]
        nm_ref[ROWS:, :] = nm1_ref[...]
        g_ref[0:ROWS, :] = g0_ref[...]
        g_ref[ROWS:, :] = g1_ref[...]
        for copy in copies:
            copy.wait()

    at = pl.ds(pl.multiple_of(step * D, D), D)
    for start in range(0, 2 * ROWS, 256):
        rows = slice(start, start + 256)
        hidden = dot_nn(nm_ref[rows, :], wup_ref[:, at])
        square = hidden * hidden
        th = jnp.tanh(hidden * (GELU_C + GELU_C * GELU_A * square))
        left = 0.5 + 0.5 * th
        active_ref[rows, :] = (hidden * left).astype(BF)
        slope = left + hidden * (0.5 - 0.5 * th * th) * (GELU_C + 3.0 * GELU_A * GELU_C * square)
        d_hidden_ref[rows, :] = (dot_nt(g_ref[rows, :], wdown_ref[at, :]) * slope).astype(BF)
    part_y = dot_nn(active_ref[...], wdown_ref[at, :])
    part_e = dot_nt(d_hidden_ref[...], wup_ref[:, at])

    @pl.when(step == 0)
    def _():
        acc_y_ref[...] = part_y
        acc_e_ref[...] = part_e

    @pl.when(step == 1)
    def _():
        e_ref[...] = (acc_e_ref[0:ROWS, :] + part_e[0:ROWS]).astype(BF)
        y_ref[...] = (acc_y_ref[0:ROWS, :] + part_y[0:ROWS]).astype(BF)
        give_e_ref[...] = (acc_e_ref[ROWS:, :] + part_e[ROWS:]).astype(BF)
        give_y_ref[...] = (acc_y_ref[ROWS:, :] + part_y[ROWS:]).astype(BF)

    part_ref[...] = dot_tn(nm_ref[...], d_hidden_ref[...]).astype(BF).reshape(16, SUB, D)
    at_half = pl.ds(pl.multiple_of(step * SUB, 16), SUB)
    for s in range(8):
        up_keep_ref[s, at_half, :] = part_ref[2 * s + side]
        up_give_ref[s, at_half, :] = part_ref[2 * s + 1 - side]
    part_ref[...] = dot_tn(active_ref[...], g_ref[...]).astype(BF).reshape(16, SUB, D)
    for z in range(2):
        for x in range(2):
            for h in range(2):
                at_h = pl.ds(h * SUB, SUB)
                row = 8 * z + 2 * x + h
                down_keep_ref[z, x, at_h, :] = part_ref[row + 4 * y_at]
                down_give_ref[z, x, at_h, :] = part_ref[row + 4 - 4 * y_at]


def mlp(where, normed, grads, pieces):
    whole = pl.BlockSpec((ROWS, D), lambda i: (0, 0))
    anywhere = pl.BlockSpec(memory_space=pl.ANY)
    return pl.pallas_call(
        mlp_kernel,
        grid=(2,),
        in_specs=[pl.BlockSpec(memory_space=pltpu.SMEM)] + [whole] * 4 + [anywhere] * 8,
        out_specs=[whole] * 4
        + [pl.BlockSpec((8, 2 * SUB, D), lambda i: (0, 0, 0))] * 2
        + [pl.BlockSpec((2, 2, FSUB, D), lambda i: (i, 0, 0, 0))] * 2,
        out_shape=[shape((ROWS, D), BF)] * 4
        + [shape((8, 2 * SUB, D), BF)] * 2
        + [shape((4, 2, FSUB, D), BF)] * 2,
        scratch_shapes=[
            pltpu.VMEM((D, FH), BF),
            pltpu.VMEM((FH, D), BF),
            pltpu.VMEM((2 * ROWS, D), BF),
            pltpu.VMEM((2 * ROWS, D), BF),
            pltpu.VMEM((2 * ROWS, D), F32),
            pltpu.VMEM((2 * ROWS, D), F32),
            pltpu.VMEM((16, SUB, D), BF),
            pltpu.VMEM((2 * ROWS, D), BF),
            pltpu.VMEM((2 * ROWS, D), BF),
            pltpu.SemaphoreType.DMA((48,)),
        ],
        compiler_params=params(),
        cost_estimate=pl.CostEstimate(
            flops=20_000_000_000, bytes_accessed=20_000_000, transcendentals=1_600_000
        ),
    )(where, *normed, *grads, *pieces)


def branch_kernel(
    mid_ref, g_ref, e0_ref, e1_ref, att_ref, w_ref, dmid_ref, datt_ref, right_ref,
    low_ref, prod_ref,
):
    gain = gain_row(w_ref[0, :, HALF:])
    wout = w_ref[0, :, D:HALF]
    for chunk in range(4):
        rows = slice(chunk * PR, (chunk + 1) * PR)
        middle = mid_ref[rows, :]
        inv = rms_inv(middle)
        unit = middle * inv
        grad = e0_ref[rows, :].astype(F32) + e1_ref[rows, :].astype(F32)
        scaled = gain * grad
        mean = jnp.mean(unit * scaled, axis=-1, keepdims=True)
        d_mid = g_ref[rows, :].astype(F32) + inv * (scaled - unit * mean)
        dmid_ref[rows, :] = d_mid
        prod_ref[rows, :] = (grad * unit).astype(BF)
        branch = d_mid.astype(BF)
        low_ref[rows, :] = branch
        datt_ref[rows, :] = dot_nt(branch, wout).astype(BF)
    right_ref[:, D:] = dot_tn(prod_ref[...], jnp.ones((ROWS, 128), BF)).astype(BF)
    right_ref[:, 0:D] = dot_tn(att_ref[...], low_ref[...]).astype(BF)


def branch(middle, d_out, own, given, attended, w_all):
    return pl.pallas_call(
        branch_kernel,
        grid=(1,),
        in_specs=[pl.BlockSpec((ROWS, D), lambda i: (0, 0))] * 5
        + [pl.BlockSpec((1, D, WIDE), lambda i: (1, 0, 0))],
        out_specs=[
            pl.BlockSpec((ROWS, D), lambda i: (0, 0)),
            pl.BlockSpec((ROWS, D), lambda i: (0, 0)),
            pl.BlockSpec((D, RIGHT), lambda i: (0, 0)),
        ],
        out_shape=[shape((ROWS, D), F32), shape((ROWS, D), BF), shape((D, RIGHT), BF)],
        scratch_shapes=[pltpu.VMEM((ROWS, D), BF), pltpu.VMEM((ROWS, D), BF)],
        compiler_params=params(),
        cost_estimate=pl.CostEstimate(
            flops=2_000_000_000, bytes_accessed=9_000_000, transcendentals=1000
        ),
    )(middle, d_out, own, given, attended, w_all)


def attn_bwd_kernel(units, *refs):
    first, last = units == (2,), units[0] == 0
    q_ref, g_ref, o_ref, r_ref, *refs = refs
    keyed = []
    for _ in units:
        keyed.append(refs[:3])
        refs = refs[3:]
    if last:
        ec_ref, kc_ref, vc_ref, *refs = refs
    if not first:
        dq_in_ref, *refs = refs
    wk_ref, wv_ref, *refs = refs
    if last:
        where_ref, wq_ref, x_ref, normed_ref, kv1_ref, kv2_ref, kv3_ref, *refs = refs
        f1_ref, f2_ref, f3_ref, right_ref, *refs = refs
        keep_ref, give_ref, f0_ref, fc_ref, *refs = refs
        late_in = (wq_ref, wk_ref, wv_ref, x_ref, normed_ref, right_ref)
        *late, sems_late = refs[:7]
        refs = refs[7:]
        wq_ref, wk_ref, wv_ref, x_ref, normed_ref, right_ref = late
        dkv_ref, dq_ref, low_ref, high_ref, prod_ref, sems, *refs = refs
    else:
        dkv_refs, refs = refs[: len(units)], refs[len(units) :]
        f_refs, refs = refs[: len(units)], refs[len(units) :]
        dq_ref, *refs = refs
    qs_ref, gs_ref, ds_ref, *refs = refs
    if last:
        sum_ref, near_ref, near_e_ref, near_qs_ref, near_gs_ref = refs
    step = pl.program_id(0)

    def late_copies():
        sources = (
            late_in[0].at[pl.ds(0, 1), :, pl.ds(0, D)],
            late_in[1].at[pl.ds(0, 1), :, pl.ds(D, D)],
            late_in[2].at[pl.ds(1, 1), :, pl.ds(0, D)],
            *late_in[3:],
        )
        return [
            pltpu.make_async_copy(source, target, sems_late.at[at])
            for at, (source, target) in enumerate(zip(sources, late))
        ]

    if last:

        @pl.when(step == 0)
        def _():
            for at, ref in enumerate((kv1_ref, kv2_ref, kv3_ref)):
                rows = pl.ds((at + 1) * UNIT, UNIT)
                pltpu.make_async_copy(ref, dkv_ref.at[:, rows, :], sems.at[at]).start()
            for copy in late_copies():
                copy.start()

    low_half = lane_half(0)
    for pair in range(2):
        lanes = slice(pair * WIDTH, (pair + 1) * WIDTH)
        lanes_v = slice((2 + pair) * WIDTH, (3 + pair) * WIDTH)
        scaled_grad = g_ref[:, lanes].astype(F32) * r_ref[:, lanes]
        prod = scaled_grad * o_ref[:, lanes].astype(F32)
        low_grad = scaled_grad.astype(BF)
        query = q_ref[:, lanes]
        deltas = []
        for head in range(2):
            half = lane_half(head)
            rows = slice(head * ROWS, (head + 1) * ROWS)
            deltas.append(jnp.sum(jnp.where(half, prod, 0.0), axis=-1, keepdims=True))
            gs_ref[rows, :] = jnp.where(half, low_grad, jnp.zeros_like(low_grad))
            qs_ref[rows, :] = jnp.where(half, query, jnp.zeros_like(query))
        delta = jnp.concatenate(deltas, axis=0)
        d_query = None
        for u, (e_ref, k_ref, v_ref) in enumerate(keyed):
            out_ref = dkv_ref if last else dkv_refs[u]
            terms = e_ref[2 * pair : 2 * pair + 2].reshape(2 * ROWS, UNIT)
            d_soft = dot_nt(gs_ref[...], v_ref[:, lanes])
            ds_ref[...] = terms * (d_soft - delta).astype(BF)
            more = dot_nn(ds_ref[...], k_ref[:, lanes])
            d_query = more if d_query is None else d_query + more
            out_ref[step, 0:UNIT, lanes] = dot_tn(ds_ref[...], qs_ref[...]).astype(BF)
            out_ref[step, 0:UNIT, lanes_v] = dot_tn(terms, gs_ref[...]).astype(BF)
        total = jnp.where(low_half, d_query[0:ROWS], d_query[ROWS:])
        if not first:
            total = total + dq_in_ref[:, lanes]
        if not last:
            dq_ref[:, lanes] = total
            continue
        sum_ref[...] = total
        for side in range(2):
            own = slice(side * PR, (side + 1) * PR)
            mine = slice((2 + side) * PR, (3 + side) * PR)
            near_q = []
            for head in range(2):
                rows = slice(head * ROWS + mine.start, head * ROWS + mine.stop)
                at = slice(head * PR, (head + 1) * PR)
                near = ec_ref[2 * pair + head, own, :]
                d_soft = dot_nt(gs_ref[rows, :], vc_ref[own, lanes])
                near_ref[at, :] = near * (d_soft - deltas[head][mine]).astype(BF)
                near_e_ref[at, :] = near
                near_qs_ref[at, :] = qs_ref[rows, :]
                near_gs_ref[at, :] = gs_ref[rows, :]
                near_q.append(dot_nn(near_ref[at, :], kc_ref[own, lanes]))
            sum_ref[mine, :] += jnp.where(low_half, near_q[0], near_q[1])
            rows = slice(PLEN + side * PR, PLEN + (side + 1) * PR)
            dkv_ref[step, rows, lanes] = dot_tn(near_ref[...], near_qs_ref[...]).astype(BF)
            dkv_ref[step, rows, lanes_v] = dot_tn(near_e_ref[...], near_gs_ref[...]).astype(BF)
        dq_ref[step, :, lanes] = (sum_ref[...] * SCALE).astype(BF)

    def back_to_rows(dkv, rows):
        grad = None
        for i in range(3):
            at = slice(i * UNIT, (i + 1) * UNIT)
            more = dot_nt(dkv[i, rows, 0:UNIT], wk_ref[0, :, at])
            more = more + dot_nt(dkv[i, rows, UNIT:], wv_ref[0, :, at])
            grad = more if grad is None else grad + more
        return grad

    @pl.when(step == pl.num_programs(0) - 1)
    def _():
        if not last:
            for dkv, f_ref in zip(dkv_refs, f_refs):
                f_ref[...] = back_to_rows(dkv, slice(0, UNIT)).astype(BF)
            return
        for at, ref in enumerate((kv1_ref, kv2_ref, kv3_ref)):
            rows = pl.ds((at + 1) * UNIT, UNIT)
            pltpu.make_async_copy(ref, dkv_ref.at[:, rows, :], sems.at[at]).wait()
        for copy in late_copies():
            copy.wait()
        high_ref[:, D:] = right_ref[...]
        for out_ref, rows, q_rows in (
            (f0_ref, slice(0, UNIT), slice(0, UNIT)),
            (fc_ref, slice(PLEN, KEYS), slice(UNIT, ROWS)),
        ):
            grad = back_to_rows(dkv_ref, rows)
            for i in range(3):
                at = slice(i * UNIT, (i + 1) * UNIT)
                grad = grad + dot_nt(dq_ref[i, q_rows, :], wq_ref[0, :, at])
            out_ref[...] = grad
        for at, f_ref in enumerate((f0_ref, f1_ref, f2_ref, f3_ref, fc_ref)):
            rows = slice(at * UNIT, (at + 1) * UNIT)
            tokens = x_ref[rows, :].astype(F32)
            prod_ref[rows, :] = (f_ref[...].astype(F32) * (tokens * rms_inv(tokens))).astype(BF)
        low_ref[:, HALF:] = dot_tn(prod_ref[...], jnp.ones((KEYS, 128), BF)).astype(BF)
        for i in range(3):
            at = slice(i * UNIT, (i + 1) * UNIT)
            low_ref[:, at] = (
                dot_tn(normed_ref[0:UNIT, :], dq_ref[i, 0:UNIT, :])
                + dot_tn(normed_ref[PLEN:, :], dq_ref[i, UNIT:, :])
            ).astype(BF)
            both = dot_tn(normed_ref[...], dkv_ref[i]).astype(BF)
            low_ref[:, D + i * UNIT : D + (i + 1) * UNIT] = both[:, 0:UNIT]
            high_ref[:, at] = both[:, UNIT:]

        for core, low_out, high_out in ((0, keep_ref, give_ref), (1, give_ref, keep_ref)):

            @pl.when(where_ref[2] == core)
            def _():
                copies = [
                    pltpu.make_async_copy(low_ref, low_out, sems.at[3]),
                    pltpu.make_async_copy(high_ref, high_out, sems.at[4]),
                ]
                for copy in copies:
                    copy.start()
                for copy in copies:
                    copy.wait()


def attn_bwd(units, saved, d_att, w_all, dq=None, rest=None):
    first, last = units == (2,), units[0] == 0
    q, k, v, e, ec, o, r = saved
    width = 2 * WIDTH
    lanes = lambda i: (0, i)
    full = lambda *dims: pl.BlockSpec(dims, lambda i: (0,) * len(dims))
    rows = pl.BlockSpec((ROWS, width), lanes)
    anywhere = pl.BlockSpec(memory_space=pl.ANY)
    weight = lambda half, at: pl.BlockSpec((1, D, D), lambda i: (half, 0, at))
    specs, args = [rows] * 4, [q, d_att, o, r]
    for u in units:
        specs += [
            pl.BlockSpec((4, ROWS, UNIT), lambda i, u=u: (i, 0, u)),
            pl.BlockSpec((UNIT, width), lambda i, u=u: (u, i)),
            pl.BlockSpec((UNIT, width), lambda i, u=u: (u, i)),
        ]
        args += [e, k, v]
    if last:
        specs += [
            pl.BlockSpec((4, UNIT, PR), lambda i: (i, 0, 0)),
            pl.BlockSpec((UNIT, width), lambda i: (4, i)),
            pl.BlockSpec((UNIT, width), lambda i: (4, i)),
        ]
        args += [ec, k, v]
    if not first:
        specs.append(rows)
        args.append(dq)
    specs += [anywhere, anywhere] if last else [weight(0, 1), weight(1, 0)]
    args += [w_all, w_all]
    kv = (3, UNIT, 2 * UNIT)
    if last:
        where, x_all, normed, kvs, fs, right = rest
        specs += [pl.BlockSpec(memory_space=pltpu.SMEM)] + [anywhere] * 6
        specs += [full(UNIT, D)] * 3 + [anywhere]
        args += [where, w_all, x_all, normed, *kvs, *fs, right]
        outs = [anywhere, anywhere, full(UNIT, D), full(UNIT, D)]
        out_shapes = [shape((D, WIDE), BF)] * 2 + [shape((UNIT, D), F32)] * 2
        scratch = [
            pltpu.VMEM((1, D, D), BF),
            pltpu.VMEM((1, D, D), BF),
            pltpu.VMEM((1, D, D), BF),
            pltpu.VMEM((KEYS, D), BF),
            pltpu.VMEM((KEYS, D), BF),
            pltpu.VMEM((D, RIGHT), BF),
            pltpu.SemaphoreType.DMA((6,)),
            pltpu.VMEM((3, KEYS, 2 * UNIT), BF),
            pltpu.VMEM((3, ROWS, UNIT), BF),
            pltpu.VMEM((D, WIDE), BF),
            pltpu.VMEM((D, WIDE), BF),
            pltpu.VMEM((KEYS, D), BF),
            pltpu.SemaphoreType.DMA((5,)),
        ]
    else:
        outs = [full(*kv)] * len(units) + [full(UNIT, D)] * len(units) + [rows]
        out_shapes = [shape(kv, BF)] * len(units) + [shape((UNIT, D), BF)] * len(units)
        out_shapes.append(shape((ROWS, D), F32))
        scratch = []
    return pl.pallas_call(
        lambda *refs: attn_bwd_kernel(units, *refs),
        grid=(3,),
        in_specs=specs,
        out_specs=outs,
        out_shape=out_shapes,
        scratch_shapes=scratch
        + [
            pltpu.VMEM((2 * ROWS, WIDTH), BF),
            pltpu.VMEM((2 * ROWS, WIDTH), BF),
            pltpu.VMEM((2 * ROWS, UNIT), BF),
        ]
        + ([pltpu.VMEM((ROWS, WIDTH), F32)] + [pltpu.VMEM((UNIT, WIDTH), BF)] * 4 if last else []),
        compiler_params=params(),
        cost_estimate=pl.CostEstimate(
            flops=10_000_000_000 * (len(units) + last), bytes_accessed=10_000_000, transcendentals=1000
        ),
    )(*args)


def tail_kernel(x_ref, f0_ref, f1_ref, f2_ref, f3_ref, fc_ref, dmid_ref, w_ref, keep_ref, give_ref):
    gain = gain_row(w_ref[0])
    for chunk in range(4):
        rows = slice(chunk * PR, (chunk + 1) * PR)
        part = x_ref[rows, :].astype(F32)
        inv = rms_inv(part)
        unit = part * inv
        if chunk < 2:
            grad = f0_ref[rows, :].astype(F32)
            for f_ref in (f1_ref, f2_ref, f3_ref):
                grad = grad + f_ref[rows, :].astype(F32)
        else:
            grad = fc_ref[(chunk - 2) * PR : (chunk - 1) * PR, :]
        scaled = gain * grad
        mean = jnp.mean(unit * scaled, axis=-1, keepdims=True)
        out_ref = give_ref if chunk % 2 else keep_ref
        at = slice(chunk // 2 * PR, (chunk // 2 + 1) * PR)
        out_ref[at, :] = (dmid_ref[rows, :] + inv * (scaled - unit * mean)).astype(out_ref.dtype)


def tail(x_own, f_parts, f_cont, d_mid, w_all):
    whole = lambda i: (0, 0)
    half = pl.BlockSpec((2 * PR, D), whole)
    full = pl.BlockSpec((ROWS, D), whole)
    return pl.pallas_call(
        tail_kernel,
        grid=(1,),
        in_specs=[full, half, half, half, half, half, full]
        + [pl.BlockSpec((1, D, 128), lambda i: (0, 0, HALF // 128))],
        out_specs=[half, half],
        out_shape=[shape((2 * PR, D), F32), shape((2 * PR, D), BF)],
        compiler_params=params(),
        cost_estimate=pl.CostEstimate(flops=20_000_000, bytes_accessed=7_000_000, transcendentals=1000),
    )(x_own, *f_parts, f_cont, d_mid, w_all)


def total_of(*parts):
    total = parts[0].astype(F32)
    for part in parts[1:]:
        total = total + part.astype(F32)
    return total.astype(BF)


def run_whole(kernel, outs, *args, dtype=BF):
    return pl.pallas_call(
        kernel,
        in_specs=[pl.BlockSpec(memory_space=pltpu.SMEM)]
        + [pl.BlockSpec(memory_space=pltpu.VMEM)] * (len(args) - 1),
        out_specs=[pl.BlockSpec(memory_space=pltpu.VMEM)] * len(outs),
        out_shape=[shape(dims, dtype) for dims in outs],
        compiler_params=params(),
        cost_estimate=pl.CostEstimate(flops=1_000_000, bytes_accessed=7_000_000, transcendentals=0),
    )(*args)


def fold_two_kernel(where_ref, a0_ref, a1_ref, b0_ref, b1_ref, ak_ref, ag_ref, bk_ref, bg_ref):
    y_at, side = where_ref[0] % 2, where_ref[1]
    for z in range(4):
        ak_ref[z] = total_of(a0_ref[z, y_at], a1_ref[z, y_at])
        ag_ref[z] = total_of(a0_ref[z, 1 - y_at], a1_ref[z, 1 - y_at])
        bk_ref[z] = total_of(b0_ref[z, side], b1_ref[z, side])
        bg_ref[z] = total_of(b0_ref[z, 1 - side], b1_ref[z, 1 - side])


def fold_rows_kernel(where_ref, a0_ref, a1_ref, b0_ref, b1_ref, *outs):
    z_at = where_ref[0] // 2
    rows = a0_ref.shape[1]
    for step, out_ref in enumerate(outs):
        z = jnp.bitwise_xor(z_at, step)
        out_ref[0:rows, :] = total_of(a0_ref[z], a1_ref[z])
        out_ref[rows:, :] = total_of(b0_ref[z], b1_ref[z])


def fold_cols_kernel(where_ref, a0_ref, a1_ref, b0_ref, b1_ref, *outs):
    z_at = where_ref[0] // 2
    cols = a0_ref.shape[2]
    for step, out_ref in enumerate(outs):
        z = jnp.bitwise_xor(z_at, step)
        out_ref[:, 0:cols] = total_of(a0_ref[z], a1_ref[z])
        out_ref[:, cols:] = total_of(b0_ref[z], b1_ref[z])


def fold_core_kernel(where_ref, own_ref, got_ref, ak_ref, ag_ref, bk_ref, bg_ref):
    y_at, side = where_ref[0] % 2, where_ref[1]
    left, right = slice(0, LEFT), slice(LEFT, WIDE)

    def block(s, x, cols):
        rows = pl.ds(pl.multiple_of((2 * s + x) * SUB, 16), SUB)
        return total_of(own_ref[rows, cols], got_ref[rows, cols])

    for s in range(8):
        ak_ref[s // 2, s % 2] = block(s, side, left)
        ag_ref[s // 2, s % 2] = block(s, 1 - side, left)
    for z in range(4):
        for x in range(2):
            bk_ref[z, x] = block(2 * z + y_at, x, right)
            bg_ref[z, x] = block(2 * z + 1 - y_at, x, right)


def unpack_kernel(where_ref, here_ref, far_ref, up_ref, down_ref):
    side, core = where_ref[1], where_ref[2]
    first = core == 0
    for x in range(2):
        at = jnp.bitwise_xor(side, x)
        rows = slice(x * SUB, (x + 1) * SUB)
        here, far = here_ref[at].astype(F32), far_ref[at].astype(F32)
        low, high = jnp.where(first, here, far), jnp.where(first, far, here)
        down_ref[x * FSUB : (x + 1) * FSUB, :] = low[2 * SUB :]
        down_ref[(2 + x) * FSUB : (3 + x) * FSUB, :] = high[2 * SUB :]
        for half in range(2):
            own = slice(half * SUB, (half + 1) * SUB)
            for i in range(4):
                cols = slice(i * 2 * FSUB, (i + 1) * 2 * FSUB)
                start = (half * 4 + i) * 4 * FSUB
                up_ref[rows, start : start + 4 * FSUB] = jnp.concatenate(
                    [low[own, cols], high[own, cols]], axis=1
                )


def finish_kernel(where_ref, own_ref, side_ref, core_ref, far_ref, qkv_ref, out_ref, gain_ref):
    first, near = where_ref[2] == 0, where_ref[1] == 0
    for x in range(2):
        mine = jnp.where(near == (x == 0), own_ref[...], side_ref[...]).astype(F32)
        theirs = jnp.where(near == (x == 0), core_ref[...], far_ref[...]).astype(F32)
        low, high = jnp.where(first, mine, theirs), jnp.where(first, theirs, mine)
        rows = slice(x * SUB, (x + 1) * SUB)
        qkv_ref[rows, 0:HALF] = low[:, 0:HALF]
        qkv_ref[rows, HALF:] = high[:, 0:D]
        out_ref[rows, :] = high[:, D:HALF]
        gain_ref[rows, 0:128] = low[:, HALF:]
        gain_ref[rows, 128:] = high[:, HALF:]


def over(axis, value, bits):
    return lax.ppermute(value, axis, [(i, i ^ bits) for i in range(lax.axis_size(axis))])


def cut(values, start, rows=PR):
    return lax.dynamic_slice_in_dim(values, start, rows, 0)


def pick(values, at):
    return lax.dynamic_index_in_dim(values, at, 0, keepdims=False)


def pick_of(values, at, axis):
    return lax.dynamic_index_in_dim(values, at, axis, keepdims=False)


def tie(*values):
    return lax.optimization_barrier(values)


def per_device(tokens, w_qkv, w_out, w_up, w_down, gain_attn, gain_mlp, d_out):
    staged = lax.axis_size("shard") == 8
    shard = lax.axis_index("shard")
    rep = lax.axis_index("rep")
    side, core = rep // 2, rep % 2
    pos = shard % 8
    y_at, z_at = pos % 2, pos // 2
    table = [pos ^ d for d in ORDER] if staged else [jnp.int32(2 * (d % 4) + d // 4) for d in range(8)]
    where = jnp.stack([pos, side, core] + [jnp.int32(0)] * 5 + table).astype(jnp.int32)

    def to_give(values):
        return jnp.concatenate([cut(values, (1 - y_at) * PR), cut(values, (3 - y_at) * PR)], axis=0)

    def own_rows(values, got):
        mine_p, mine_c = cut(values, y_at * PR), cut(values, (2 + y_at) * PR)
        return jnp.concatenate([mine_p, got[:PR], mine_c, got[PR:]], axis=0)

    def to_return(values):
        return jnp.concatenate([values[PR : 2 * PR], values[3 * PR :]], axis=0)

    def home_rows(keep_p, keep_c, got):
        got = got.astype(keep_p.dtype)
        first = y_at == 0
        return jnp.concatenate(
            [
                jnp.where(first, keep_p, got[:PR]),
                jnp.where(first, got[:PR], keep_p),
                jnp.where(first, keep_c, got[PR:]),
                jnp.where(first, got[PR:], keep_c),
            ],
            axis=0,
        )

    def halves(qkv, out, gain_a, gain_m):
        wide = lambda gain: jnp.broadcast_to(gain[:, None], (gain.shape[0], 128))
        return (
            jnp.concatenate([qkv[:, :HALF], wide(gain_a)], axis=1),
            jnp.concatenate([qkv[:, HALF:], out, wide(gain_m)], axis=1),
        )

    def half_up(up):
        return pick_of(up.reshape(up.shape[0], 8, 2, 2 * FSUB), core, 2).reshape(up.shape[0], FH)

    def own_up(up):
        mine = half_up(cut(up, side * SUB, SUB))
        return jnp.concatenate([mine[:, :D], mine[:, D:]], axis=0)

    if staged:
        low, high = halves(w_qkv, w_out, gain_attn, gain_mlp)
        own_piece = cut(jnp.where(core == 0, low, high), side * SUB, SUB)
        own_mlp = jnp.concatenate(
            [own_up(w_up), cut(w_down, core * 2 * FSUB + side * FSUB, FSUB)], axis=0
        )
        t_got, z1, z2, z3 = tie(
            over("shard", to_give(tokens), 1),
            *[over("shard", own_piece, k) for k in (2, 4, 6)],
        )
        x_own = own_rows(tokens, t_got)
        near = x_own[: 2 * PR]
        line = (own_piece, z1, z2, z3)
        left = jnp.stack([part[:, :LEFT] for part in line])
        right = jnp.stack([part[:, LEFT:] for part in line])
        own_mlp, left, right, near = tie(own_mlp, left, right, near)
        m1, m2, m3, left_y, right_x, g_got = tie(
            *[over("shard", own_mlp, k) for k in (2, 4, 6)],
            over("shard", left, 1),
            over("rep", right, 2),
            over("shard", to_give(d_out), 1),
        )
        left = jnp.concatenate([left, left_y], axis=0)
        right = jnp.concatenate([right, right_x], axis=0)
        mlp_line = (own_mlp, m1, m2, m3)
        up = jnp.stack([part[: 2 * SUB] for part in mlp_line])
        down = jnp.stack([part[2 * SUB :] for part in mlp_line])
        near, left, right, up, down = tie(near, left, right, up, down)
        near1, near2, near3, left_x, right_y, up_y, down_x = tie(
            *[over("shard", near, k) for k in (2, 4, 6)],
            over("rep", left, 2),
            over("shard", right, 1),
            over("shard", up, 1),
            over("rep", down, 2),
        )
        pieces = tie(
            left, left_x, over("rep", left, 1), over("rep", left_x, 1),
            right, right_y, over("rep", right, 1), over("rep", right_y, 1),
        )
        up, up_y, down, down_x, pieces = tie(up, up_y, down, down_x, pieces)
        mlp_pieces = (
            up, over("rep", up, 2), up_y, over("rep", up_y, 2),
            down, down_x, over("shard", down, 1), over("shard", down_x, 1),
        )
    else:
        gathered = [
            lax.all_gather(w, "shard", axis=0, tiled=True)
            for w in (w_qkv, w_out, gain_attn, gain_mlp, w_up, w_down)
        ]
        natural = jnp.stack(halves(*gathered[:4])).reshape(2, 4, 2, 2, SUB, WIDE)
        pieces = []
        for dc in (0, 1):
            by_core = pick(natural, core ^ dc)
            for dx in (0, 1):
                both = pick_of(by_core[..., :LEFT], side ^ dx, 2)
                pieces.append(jnp.concatenate([both[:, 0], both[:, 1]], axis=0))
        for dc in (0, 1):
            by_core = pick(natural, core ^ dc)[..., LEFT:]
            for dy in (0, 1):
                both = [pick_of(by_core[:, dy], side ^ dx, 1) for dx in (0, 1)]
                pieces.append(jnp.concatenate(both, axis=0))
        pieces = tuple(pieces)
        up = half_up(gathered[4]).reshape(4, 2, 2, SUB, 2, D).transpose(1, 0, 2, 4, 3, 5)
        up = up.reshape(2, 4, 2, 2 * SUB, D)
        down = pick_of(gathered[5].reshape(4, 2, 2, 2, FSUB, D), core, 2).transpose(1, 0, 2, 3, 4)
        mlp_pieces = tuple(
            pick_of(both[dy], side ^ dx, 1) for both in (up, down) for dy in (0, 1) for dx in (0, 1)
        )
        x_own = own_rows(tokens, over("shard", to_give(tokens), 1))
        near = x_own[: 2 * PR]
        near1, near2, near3 = [over("shard", near, k) for k in (2, 4, 6)]
        g_got = over("shard", to_give(d_out), 1)
    x_all = jnp.concatenate([near, near1, near2, near3, x_own[2 * PR :]], axis=0)
    g_own = own_rows(d_out, g_got)
    x_all, g_own = tie(x_all, g_own)

    g_core = over("rep", g_own, 1)
    forward = attn_fwd(where, x_all, pieces)
    forward, mlp_pieces, g_core = tie(forward, mlp_pieces, g_core)
    w_all, q, k, v, e, ec, attended, inv_sum, middle, nm, normed = forward

    nm_core, nm = tie(over("rep", nm, 1), nm)
    e_own, y_own, e_give, y_give, *mlp_grads = mlp(
        where, (nm, nm_core), (g_own, g_core), mlp_pieces
    )
    e_got, y_give, mlp_grads = tie(over("rep", e_give, 1), y_give, mlp_grads)
    up_keep, up_give, down_keep, down_give = mlp_grads
    y_got = over("rep", y_give, 1)
    if staged:
        up_got, down_got = over("rep", up_give, 2), over("shard", down_give, 1)
    d_mid, d_att, d_right = branch(middle, g_own, e_own, e_got, attended, w_all)

    saved = (q, k, v, e, ec, attended, inv_sum)
    kv2, f2_give, dq = attn_bwd((2,), saved, d_att, w_all)
    y_got, dq = tie(y_got, dq)
    block_rows = (middle + y_own.astype(F32) + y_got.astype(F32)).astype(BF)
    block_give = to_return(block_rows)
    f2_give, dq, block_give = tie(f2_give, dq, block_give)
    f2 = over("shard", f2_give, 4)
    kv3, kv1, f3_give, f1_give, dq = attn_bwd((3, 1), saved, d_att, w_all, dq)
    f2, f3_give, f1_give, dq, block_give = tie(f2, f3_give, f1_give, dq, block_give)
    if staged:
        up_got, down_got, dq = tie(up_got, down_got, dq)
        by_pair = (4, 2, 2 * SUB, D)
        folded = run_whole(
            fold_two_kernel, [(4, 2 * SUB, D)] * 4, where,
            up_keep.reshape(by_pair), up_got.reshape(by_pair), down_keep, down_got,
        )
        (up_keep, up_give, down_keep, down_give), dq, f3_give, f1_give, block_give = tie(
            folded, dq, f3_give, f1_give, block_give
        )
        up_got, down_got = over("shard", up_give, 1), over("rep", down_give, 2)
    f1, f3, b_got = over("shard", f1_give, 2), over("shard", f3_give, 6), over("shard", block_give, 1)
    keep, give, f0, f_cont = attn_bwd(
        (0,), saved, d_att, w_all, dq,
        (where, x_all, normed, (kv1, kv2, kv3), (f1_give, f2_give, f3_give), d_right),
    )
    f1, f3, b_got, keep, give, f0, f_cont = tie(f1, f3, b_got, keep, give, f0, f_cont)
    if staged:
        up_got, down_got, give = tie(up_got, down_got, give)
        mlp_total, *mlp_gives = run_whole(
            fold_rows_kernel, [(4 * SUB, D)] * 4, where, up_keep, up_got, down_keep, down_got
        )
        chip_got, mlp_gives = tie(over("rep", give, 1), mlp_gives)
        left, right = (4, 2, SUB, LEFT), (4, 2, SUB, WIDE - LEFT)
        left_keep, left_give, right_keep, right_give = run_whole(
            fold_core_kernel, [left, left, right, right], where, keep, chip_got
        )
        left_give, right_give, mlp_gives, f0 = tie(left_give, right_give, mlp_gives, f0)
        left_got, right_got, m2, mlp_gives, token_keep, token_give = tie(
            over("rep", left_give, 2),
            over("shard", right_give, 1),
            over("shard", mlp_gives[1], 4),
            mlp_gives,
            *tail(x_own, (f0, f1, f2, f3), f_cont, d_mid, w_all),
        )
        left_keep, left_give, right_keep, right_give = run_whole(
            fold_two_kernel,
            [(4, SUB, LEFT)] * 2 + [(4, SUB, WIDE - LEFT)] * 2,
            where, left_keep, left_got, right_keep, right_got,
        )
        left_got, right_got, m1, m3 = tie(
            over("shard", left_give, 1),
            over("rep", right_give, 2),
            over("shard", mlp_gives[0], 2),
            over("shard", mlp_gives[2], 6),
        )
        total, *gives = run_whole(
            fold_cols_kernel, [(SUB, WIDE)] * 4, where, left_keep, left_got, right_keep, right_got
        )
        gives, m1, m3 = tie(gives, m1, m3)
        mlp_total = total_of(mlp_total, m1, m2, m3)
        z1, z2, z3, m_got, mlp_total, t_got = tie(
            *[over("shard", gives[step - 1], 2 * step) for step in (1, 2, 3)],
            over("rep", mlp_total, 2),
            mlp_total,
            over("shard", token_give, 1),
        )
        total = total_of(total, z1, z2, z3)
        by_side = jnp.stack([mlp_total, m_got])
        other, core_got, m_got, by_side = tie(
            over("rep", total, 2), over("rep", total, 1), over("rep", by_side, 1), by_side
        )
        far = over("rep", other, 1)
        d_wup, d_wdown = run_whole(
            unpack_kernel, [(2 * SUB, FF), (4 * FSUB, D)], where, by_side, m_got, dtype=F32
        )
        d_wqkv, d_wout, d_gains = run_whole(
            finish_kernel, [(2 * SUB, 3 * D), (2 * SUB, D), (2 * SUB, 256)],
            where, total, other, core_got, far, dtype=F32,
        )
        d_gain_attn, d_gain_mlp = d_gains[:, 0], d_gains[:, 128]
    else:
        token_keep, token_give = tail(x_own, (f0, f1, f2, f3), f_cont, d_mid, w_all)
        t_got = over("shard", token_give, 1)
        low, high = jnp.where(core == 0, keep, give), jnp.where(core == 0, give, keep)

        def by_side_of(keep, give, at):
            first = at == 0
            return jnp.stack([jnp.where(first, keep, give), jnp.where(first, give, keep)])

        up = by_side_of(up_keep, up_give, side).reshape(2, 8, 2, SUB, D)
        up = up.transpose(1, 0, 3, 2, 4).reshape(D, 8, 1, 2 * FSUB)
        down = by_side_of(down_keep, down_give, y_at).transpose(1, 0, 2, 3, 4)
        down = down.reshape(8, 1, 2 * FSUB, D)
        peer_up, peer_down = over("rep", up, 1), over("rep", down, 1)
        first = core == 0
        up, peer_up = jnp.where(first, up, peer_up), jnp.where(first, peer_up, up)
        down, peer_down = jnp.where(first, down, peer_down), jnp.where(first, peer_down, down)
        up = jnp.concatenate([up, peer_up], axis=2).reshape(D, FF)
        down = jnp.concatenate([down, peer_down], axis=1).reshape(FF, D)
        rest = lambda v: (v.astype(F32) + over("rep", v, 2).astype(F32)).astype(BF)
        up, down = rest(up), rest(down)
        scatter = lambda v: lax.psum_scatter(v, "shard", scatter_dimension=0, tiled=True)
        d_wup, d_wdown = scatter(up).astype(F32), scatter(down).astype(F32)
        low = lax.psum(scatter(low), "rep").astype(F32)
        high = lax.psum(scatter(high), "rep").astype(F32)
        d_wqkv = jnp.concatenate([low[:, :HALF], high[:, :D]], axis=1)
        d_wout, d_gain_attn, d_gain_mlp = high[:, D:HALF], low[:, HALF], high[:, HALF]

    return (
        home_rows(block_rows[:PR], block_rows[2 * PR : 3 * PR], b_got),
        home_rows(token_keep[:PR], token_keep[PR:], t_got),
        d_wqkv,
        d_wout,
        d_wup,
        d_wdown,
        d_gain_attn,
        d_gain_mlp,
    )


def solution(mesh):
    weights = P("shard", None)
    rows = P(("rep", "shard"), None)
    return jax.shard_map(
        per_device,
        mesh=mesh,
        in_specs=(rows, weights, weights, weights, weights, P("shard"), P("shard"), rows),
        out_specs=(rows, rows, weights, weights, weights, weights, P("shard"), P("shard")),
        check_vma=False,
    )
```

profile of v0, /device:TPU:0, one launch (start us, length us, event | category | flops | bytes accessed | tf_op | source)
XLA Modules:
  0.0 336.8 jit_solution(10159472246566317701)
XLA Ops:
  5.1 5.1 %collective-permute-start.3 = (bf16[48,1664]{1,0:T(8,128)(2,1)S(1)}, bf16[48,1664]{1,0:T(8,128)(2,1)}, u32[]{:S(2)}, u32[]{:S(2)}) collective-permute-start(bf16[48,1664]{1,0:T(8,128)(2,1)S(1)} %fusion.2), channel_id=1, source_target_pairs={{0,6},{1,7},{2,4},{3,5},{4,2},{5,3},{6,0},{7,1},{8,14},{9,15},{10,... | collective-permute-start | bytes 479240 | tf_op jit(solution)/shard_map/ppermute | solution.py:806
  18.0 5.9 %collective-permute-done.2 = bf16[48,1664]{1,0:T(8,128)(2,1)} collective-permute-done((bf16[48,1664]{1,0:T(8,128)(2,1)S(1)}, bf16[48,1664]{1,0:T(8,128)(2,1)}, u32[]{:S(2)}, u32[]{:S(2)}) %collective-permute-start.2) | collective-permute-done | bytes 159776 | tf_op jit(solution)/shard_map/ppermute | solution.py:806
  34.9 3.6 %collective-permute-start.6 = (bf16[192,768]{1,0:T(8,128)(2,1)S(1)}, bf16[192,768]{1,0:T(8,128)(2,1)S(1)}, u32[]{:S(2)}, u32[]{:S(2)}) collective-permute-start(bf16[192,768]{1,0:T(8,128)(2,1)S(1)} %pad_maximum_fusion.14), channel_id=1, source_target_pairs={{0,6},{1,7},{2,4},{3,5},{4,2},{5,3},{6,0},{7,1},{8,14},{9,15},{10,... | collective-permute-start | bytes 884744 | tf_op jit(solution)/shard_map/ppermute | solution.py:806
  40.2 6.5 %collective-permute-done.6 = bf16[192,768]{1,0:T(8,128)(2,1)S(1)} collective-permute-done((bf16[192,768]{1,0:T(8,128)(2,1)S(1)}, bf16[192,768]{1,0:T(8,128)(2,1)S(1)}, u32[]{:S(2)}, u32[]{:S(2)}) %collective-permute-start.6) | collective-permute-done | bytes 294944 | tf_op jit(solution)/shard_map/ppermute | solution.py:806
  46.7 12.8 %collective-permute-done.5 = bf16[192,768]{1,0:T(8,128)(2,1)S(1)} collective-permute-done((bf16[192,768]{1,0:T(8,128)(2,1)S(1)}, bf16[192,768]{1,0:T(8,128)(2,1)S(1)}, u32[]{:S(2)}, u32[]{:S(2)}) %collective-permute-start.5) | collective-permute-done | bytes 294944 | tf_op jit(solution)/shard_map/ppermute | solution.py:806
  67.3 9.0 %collective-permute-done.12 = bf16[256,768]{1,0:T(8,128)(2,1)S(1)} collective-permute-done((bf16[256,768]{1,0:T(8,128)(2,1)S(1)}, bf16[256,768]{1,0:T(8,128)(2,1)S(1)}, u32[]{:S(2)}, u32[]{:S(2)}) %collective-permute-start.12) | collective-permute-done | bytes 393248 | tf_op jit(solution)/shard_map/ppermute | solution.py:806
  77.5 18.0 %collective-permute-done.11 = bf16[256,768]{1,0:T(8,128)(2,1)S(1)} collective-permute-done((bf16[256,768]{1,0:T(8,128)(2,1)S(1)}, bf16[256,768]{1,0:T(8,128)(2,1)S(1)}, u32[]{:S(2)}, u32[]{:S(2)}) %collective-permute-start.11) | collective-permute-done | bytes 393248 | tf_op jit(solution)/shard_map/ppermute | solution.py:806
  96.4 7.5 %collective-permute-done.10 = bf16[256,768]{1,0:T(8,128)(2,1)S(1)} collective-permute-done((bf16[256,768]{1,0:T(8,128)(2,1)S(1)}, bf16[256,768]{1,0:T(8,128)(2,1)S(1)}, u32[]{:S(2)}, u32[]{:S(2)}) %collective-permute-start.10) | collective-permute-done | bytes 393248 | tf_op jit(solution)/shard_map/ppermute | solution.py:806
  114.9 31.4 %shard_map.143 = (bf16[2,768,1664]{2,1,0:T(8,128)(2,1)}, bf16[512,768]{1,0:T(8,128)(2,1)}, bf16[1280,768]{1,0:T(8,128)(2,1)}, bf16[1280,768]{1,0:T(8,128)(2,1)},...) custom-call(s32[16]{0:T(128)} %stack.113.where_ref.refs_13_, ...), custom_call_target="tpu_custom_call" | custom-call | flops 30000001024 | bytes 30000000 | tf_op jit(solution)/shard_map/pallas_call | solution.py:221
  149.9 24.0 %shard_map.144 = (bf16[512,768]{1,0:T(8,128)(2,1)}, bf16[512,768]{1,0:T(8,128)(2,1)}, bf16[512,768]{1,0:T(8,128)(2,1)}, bf16[512,768]{1,0:T(8,128)(2,1)}, bf16[8...) custom-call(s32[16]{0:T(128)} %stack.113.where_ref.refs_13_, ...), custom_call_target="tpu_custom_call" | custom-call | flops 20000000000 | bytes 20000000 | tf_op jit(solution)/shard_map/pallas_call | solution.py:358
  177.7 7.0 %shard_map.145 = (f32[512,768]{1,0:T(8,128)}, bf16[512,768]{1,0:T(8,128)(2,1)}, bf16[768,896]{1,0:T(8,128)(2,1)}) custom-call(f32[512,768]{1,0:T(8,128)} %get-tuple-element.271.mid_ref, bf16[512,768]{1,0:T(8,128)(2,1)} %copy-done.3, bf16[512,768]{1,0:T(8,128)(2,1)} %get-tuple-element.293.e0_ref, bf16[512,768]{1,0:T(8,128)(2,1)} %copy-done.6, ...), custom_call_target="tpu_custom_call" | custom-call | flops 2000000000 | bytes 9000000 | tf_op jit(solution)/shard_map/pallas_call | solution.py:412
  184.7 10.8 %shard_map.146 = (bf16[3,256,512]{2,1,0:T(8,128)(2,1)}, bf16[256,768]{1,0:T(8,128)(2,1)}, f32[512,768]{1,0:T(8,128)}) custom-call(bf16[512,768]{1,0:T(8,128)(2,1)} %get-tuple-element.292.refs_0_, bf16[512,768]{1,0:T(8,128)(2,1)} %get-tuple-element.297.refs_1_, bf16[512,768]{1,0:T(8,128)(2,1)} %get-tuple-element.295.att_ref.refs_2_, ...), custom_call_target="tpu_custom_call" | custom-call | flops 10000000000 | bytes 10000000 | tf_op jit(solution)/shard_map/pallas_call | solution.py:652
  198.2 16.2 %shard_map.147 = (bf16[3,256,512]{2,1,0:T(8,128)(2,1)}, bf16[3,256,512]{2,1,0:T(8,128)(2,1)}, bf16[256,768]{1,0:T(8,128)(2,1)}, bf16[256,768]{1,0:T(8,128)(2,1)}, f32[512,768]{1,0:T(8,128)}) custom-call(bf16[512,768]{1,0:T(8,128)(2,1)} %get-tuple-element.292.refs_0_, bf16[512,768]{1,0:T(8,128)(2,1)} %get-tuple-element.297.refs_1_, ...), custom_call_target="tpu_custom_call" | custom-call | flops 20000000000 | bytes 10000000 | tf_op jit(solution)/shard_map/pallas_call | solution.py:652
  214.4 3.5 %collective-permute-done.31.f2_ref = bf16[256,768]{1,0:T(8,128)(2,1)S(1)} collective-permute-done((bf16[256,768]{1,0:T(8,128)(2,1)S(1)}, bf16[256,768]{1,0:T(8,128)(2,1)S(1)}, u32[]{:S(2)}, u32[]{:S(2)}) %collective-permute-start.31) | collective-permute-done | bytes 393248 | tf_op jit(solution)/shard_map/ppermute | solution.py:806
  218.9 4.3 %shard_map.148 = (bf16[4,96,768]{2,1,0:T(8,128)(2,1)}, bf16[4,96,768]{2,1,0:T(8,128)(2,1)}, bf16[4,96,768]{2,1,0:T(8,128)(2,1)}, bf16[4,96,768]{2,1,0:T(8,128)(2,1)}) custom-call(s32[16]{0:T(128)} %stack.113.where_ref.refs_13_, bf16[4,2,96,768]{3,2,1,0:T(8,128)(2,1)} %bitcast.46, bf16[4,2,96,768]{3,2,1,0:T(8,128)(2,1)} %bitcast.47, ...), custom_call_target="tpu_custom_call" | custom-call | flops 1000000 | bytes 7000000 | tf_op jit(solution)/shard_map/pallas_call | solution.py:716
  228.3 23.1 %shard_map.149 = (bf16[768,1664]{1,0:T(8,128)(2,1)}, bf16[768,1664]{1,0:T(8,128)(2,1)}, f32[256,768]{1,0:T(8,128)}, f32[256,768]{1,0:T(8,128)}) custom-call(bf16[512,768]{1,0:T(8,128)(2,1)} %get-tuple-element.292.refs_0_, bf16[512,768]{1,0:T(8,128)(2,1)} %get-tuple-element.297.refs_1_, bf16[512,768]{1,0:T(8,128)(2,1)} %get-tuple-element.295.att_ref.refs_2_, ...), custom_call_target="tpu_custom_call" | custom-call | flops 20000000000 | bytes 10000000 | tf_op jit(solution)/shard_map/pallas_call | solution.py:652
  256.8 4.6 %shard_map.151 = (bf16[4,2,48,896]{3,2,1,0:T(8,128)(2,1)}, bf16[4,2,48,896]{3,2,1,0:T(8,128)(2,1)}, bf16[4,2,48,768]{3,2,1,0:T(8,128)(2,1)}, bf16[4,2,48,768]{3,2,1,0:T(8,128)(2,1)}) custom-call(s32[16]{0:T(128)} %stack.113.where_ref.refs_13_, bf16[768,1664]{1,0:T(8,128)(2,1)} %get-tuple-element.342.own_ref, bf16[768,1664]{1,0:T(8,128)(2,1)} %collective-permute-done.37.got_ref), custom_call_target="tpu_custom_call" | custom-call | flops 1000000 | bytes 7000000 | tf_op jit(solution)/shard_map/pallas_call | solution.py:716
  266.2 4.3 %shard_map.152 = (f32[256,768]{1,0:T(8,128)}, bf16[256,768]{1,0:T(8,128)(2,1)}) custom-call(bf16[512,768]{1,0:T(8,128)(2,1)} %pad_maximum_fusion.3.x_ref, f32[256,768]{1,0:T(8,128)} %get-tuple-element.366.f0_ref, bf16[256,768]{1,0:T(8,128)(2,1)} %copy-done.18, bf16[256,768]{1,0:T(8,128)(2,1)} %copy-done.17, bf16[256,768]{1,0:T(8,128)(2,1)} %copy-done.19, ...), custom_call_target="tpu_custom_call" | custom-call | flops 20000000 | bytes 7000000 | tf_op jit(solution)/shard_map/pallas_call | solution.py:696
  270.5 8.8 %collective-permute-done.40 = bf16[192,768]{1,0:T(8,128)(2,1)} collective-permute-done((bf16[192,768]{1,0:T(8,128)(2,1)S(1)}, bf16[192,768]{1,0:T(8,128)(2,1)}, u32[]{:S(2)}, u32[]{:S(2)}) %collective-permute-start.40) | collective-permute-done | bytes 294944 | tf_op jit(solution)/shard_map/ppermute | solution.py:806
  288.9 3.6 %collective-permute-done.42.b1_ref = bf16[4,48,768]{2,1,0:T(8,128)(2,1)S(1)} collective-permute-done((bf16[4,48,768]{2,1,0:T(8,128)(2,1)}, bf16[4,48,768]{2,1,0:T(8,128)(2,1)S(1)}, u32[]{:S(2)}, u32[]{:S(2)}) %collective-permute-start.42) | collective-permute-done | bytes 294944 | tf_op jit(solution)/shard_map/ppermute | solution.py:806
  294.6 5.9 %collective-permute-done.44 = bf16[192,768]{1,0:T(8,128)(2,1)S(1)} collective-permute-done((bf16[192,768]{1,0:T(8,128)(2,1)}, bf16[192,768]{1,0:T(8,128)(2,1)S(1)}, u32[]{:S(2)}, u32[]{:S(2)}) %collective-permute-start.44) | collective-permute-done | bytes 294944 | tf_op jit(solution)/shard_map/ppermute | solution.py:806
  310.3 4.0 %collective-permute-done.45 = bf16[48,1664]{1,0:T(8,128)(2,1)S(1)} collective-permute-done((bf16[48,1664]{1,0:T(8,128)(2,1)}, bf16[48,1664]{1,0:T(8,128)(2,1)S(1)}, u32[]{:S(2)}, u32[]{:S(2)}) %collective-permute-start.45) | collective-permute-done | bytes 159776 | tf_op jit(solution)/shard_map/ppermute | solution.py:806
  314.4 4.5 %collective-permute-done.46 = bf16[48,1664]{1,0:T(8,128)(2,1)S(1)} collective-permute-done((bf16[48,1664]{1,0:T(8,128)(2,1)}, bf16[48,1664]{1,0:T(8,128)(2,1)S(1)}, u32[]{:S(2)}, u32[]{:S(2)}) %collective-permute-start.46) | collective-permute-done | bytes 159776 | tf_op jit(solution)/shard_map/ppermute | solution.py:806
  323.6 3.6 %collective-permute-done.50.side_ref = bf16[48,1664]{1,0:T(8,128)(2,1)S(1)} collective-permute-done((bf16[48,1664]{1,0:T(8,128)(2,1)S(1)}, bf16[48,1664]{1,0:T(8,128)(2,1)S(1)}, u32[]{:S(2)}, u32[]{:S(2)}) %collective-permute-start.50) | collective-permute-done | bytes 159776 | tf_op jit(solution)/shard_map/ppermute | solution.py:806
  (240 shorter events, 107.1 us)
Async XLA Ops:
  14.6 24.0 %collective-permute-start.9 = (bf16[256,768]{1,0:T(8,128)(2,1)S(1)}, bf16[256,768]{1,0:T(8,128)(2,1)S(1)}, u32[]{:S(2)}, u32[]{:S(2)}) collective-permute-start(bf16[256,768]{1,0:T(8,128)(2,1)S(1)} %pad_maximum_fusion.11), channel_id=1, source_target_pairs={{0,1},{1,0},{2,3},{3,2},{4,5},{5,4},{6,7},{7,6},{8,9},{9,8},{10,11... | collective-permute-start | bytes 1179656 | tf_op jit(solution)/shard_map/ppermute | solution.py:806
  31.7 27.8 %collective-permute-start.7 = (bf16[4,48,896]{2,1,0:T(8,128)(2,1)S(1)}, bf16[4,48,896]{2,1,0:T(8,128)(2,1)S(1)}, u32[]{:S(2)}, u32[]{:S(2)}) collective-permute-start(bf16[4,48,896]{2,1,0:T(8,128)(2,1)S(1)} %pad_maximum_fusion.13), channel_id=1, source_target_pairs={{0,1},{1,0},{2,3},{3,2},{4,5},{5,4},{6,7},{7,6},{8,9},{9,8},{10,11... | collective-permute-start | bytes 1032200 | tf_op jit(solution)/shard_map/ppermute | solution.py:806
  38.5 21.0 %collective-permute-start.5 = (bf16[192,768]{1,0:T(8,128)(2,1)S(1)}, bf16[192,768]{1,0:T(8,128)(2,1)S(1)}, u32[]{:S(2)}, u32[]{:S(2)}) collective-permute-start(bf16[192,768]{1,0:T(8,128)(2,1)S(1)} %pad_maximum_fusion.14), channel_id=1, source_target_pairs={{0,4},{1,5},{2,6},{3,7},{4,0},{5,1},{6,2},{7,3},{8,12},{9,13},{10,... | collective-permute-start | bytes 884744 | tf_op jit(solution)/shard_map/ppermute | solution.py:806
  38.5 21.0 %collective-permute-start.4 = (bf16[192,768]{1,0:T(8,128)(2,1)S(1)}, bf16[192,768]{1,0:T(8,128)(2,1)S(1)}, u32[]{:S(2)}, u32[]{:S(2)}) collective-permute-start(bf16[192,768]{1,0:T(8,128)(2,1)S(1)} %pad_maximum_fusion.14), channel_id=1, source_target_pairs={{0,2},{1,3},{2,0},{3,1},{4,6},{5,7},{6,4},{7,5},{8,10},{9,11},{10,... | collective-permute-start | bytes 884744 | tf_op jit(solution)/shard_map/ppermute | solution.py:806
  64.8 30.7 %collective-permute-start.11 = (bf16[256,768]{1,0:T(8,128)(2,1)S(1)}, bf16[256,768]{1,0:T(8,128)(2,1)S(1)}, u32[]{:S(2)}, u32[]{:S(2)}) collective-permute-start(bf16[256,768]{1,0:T(8,128)(2,1)S(1)} %pad_maximum_fusion.10), channel_id=1, source_target_pairs={{0,4},{1,5},{2,6},{3,7},{4,0},{5,1},{6,2},{7,3},{8,12},{9,13},{10,... | collective-permute-start | bytes 1179656 | tf_op jit(solution)/shard_map/ppermute | solution.py:806
  64.8 39.7 %collective-permute-start.13 = (bf16[8,48,896]{2,1,0:T(8,128)(2,1)S(1)}, bf16[8,48,896]{2,1,0:T(8,128)(2,1)}, u32[]{:S(2)}, u32[]{:S(2)}) collective-permute-start(bf16[8,48,896]{2,1,0:T(8,128)(2,1)S(1)} %pad_maximum_fusion.4.l00_ref), channel_id=1, source_target_pairs={{0,16},{8,24},{16,0},{24,8},{1,17},{9,25},{17,1},{25,9},{2,18},{10... | collective-permute-start | bytes 2064392 | tf_op jit(solution)/shard_map/ppermute | solution.py:806
  65.3 38.6 %collective-permute-start.15 = (bf16[4,96,768]{2,1,0:T(8,128)(2,1)}, bf16[4,96,768]{2,1,0:T(8,128)(2,1)}, u32[]{:S(2)}, u32[]{:S(2)}) collective-permute-start(bf16[4,96,768]{2,1,0:T(8,128)(2,1)} %pad_maximum_fusion.6.up00_ref), channel_id=1, source_target_pairs={{0,1},{1,0},{2,3},{3,2},{4,5},{5,4},{6,7},{7,6},{8,9},{9,8},{10,11... | collective-permute-start | bytes 1769480 | tf_op jit(solution)/shard_map/ppermute | solution.py:806
  65.8 38.6 %collective-permute-start.16 = (bf16[4,96,768]{2,1,0:T(8,128)(2,1)}, bf16[4,96,768]{2,1,0:T(8,128)(2,1)}, u32[]{:S(2)}, u32[]{:S(2)}) collective-permute-start(bf16[4,96,768]{2,1,0:T(8,128)(2,1)} %pad_maximum_fusion.7.down00_ref), channel_id=1, source_target_pairs={{0,16},{8,24},{16,0},{24,8},{1,17},{9,25},{17,1},{25,9},{2,18},{10... | collective-permute-start | bytes 1769480 | tf_op jit(solution)/shard_map/ppermute | solution.py:806
  76.3 28.1 %collective-permute-start.14 = (bf16[8,48,768]{2,1,0:T(8,128)(2,1)}, bf16[8,48,768]{2,1,0:T(8,128)(2,1)}, u32[]{:S(2)}, u32[]{:S(2)}) collective-permute-start(bf16[8,48,768]{2,1,0:T(8,128)(2,1)} %pad_maximum_fusion.5.r00_ref), channel_id=1, source_target_pairs={{0,1},{1,0},{2,3},{3,2},{4,5},{5,4},{6,7},{7,6},{8,9},{9,8},{10,11... | collective-permute-start | bytes 1769480 | tf_op jit(solution)/shard_map/ppermute | solution.py:806
  107.7 38.6 %collective-permute-start.25 = (bf16[512,768]{1,0:T(8,128)(2,1)S(1)}, bf16[512,768]{1,0:T(8,128)(2,1)S(1)}, u32[]{:S(2)}, u32[]{:S(2)}) collective-permute-start(bf16[512,768]{1,0:T(8,128)(2,1)S(1)} %pad_maximum_fusion.1.g0_ref.g_ref), channel_id=1, source_target_pairs={{0,8},{8,0},{16,24},{24,16},{1,9},{9,1},{17,25},{25,17},{2,10},{10... | collective-permute-start | bytes 2359304 | tf_op jit(solution)/shard_map/ppermute | solution.py:806
  110.9 35.5 %collective-permute-start.21 = (bf16[4,96,768]{2,1,0:T(8,128)(2,1)}, bf16[4,96,768]{2,1,0:T(8,128)(2,1)S(1)}, u32[]{:S(2)}, u32[]{:S(2)}) collective-permute-start(bf16[4,96,768]{2,1,0:T(8,128)(2,1)} %pad_maximum_fusion.6.up00_ref), channel_id=1, source_target_pairs={{0,16},{8,24},{16,0},{24,8},{1,17},{9,25},{17,1},{25,9},{2,18},{10... | collective-permute-start | bytes 1769480 | tf_op jit(solution)/shard_map/ppermute | solution.py:806
  111.4 35.0 %collective-permute-start.22 = (bf16[4,96,768]{2,1,0:T(8,128)(2,1)}, bf16[4,96,768]{2,1,0:T(8,128)(2,1)S(1)}, u32[]{:S(2)}, u32[]{:S(2)}) collective-permute-start(bf16[4,96,768]{2,1,0:T(8,128)(2,1)} %collective-permute-done.15.up01_ref), channel_id=1, source_target_pairs={{0,16},{8,24},{16,0},{24,8},{1,17},{9,25},{17,1},{25,9},{2,18},{10... | collective-permute-start | bytes 1769480 | tf_op jit(solution)/shard_map/ppermute | solution.py:806
  112.9 33.5 %collective-permute-start.23 = (bf16[4,96,768]{2,1,0:T(8,128)(2,1)}, bf16[4,96,768]{2,1,0:T(8,128)(2,1)S(1)}, u32[]{:S(2)}, u32[]{:S(2)}) collective-permute-start(bf16[4,96,768]{2,1,0:T(8,128)(2,1)} %pad_maximum_fusion.7.down00_ref), channel_id=1, source_target_pairs={{0,1},{1,0},{2,3},{3,2},{4,5},{5,4},{6,7},{7,6},{8,9},{9,8},{10,11... | collective-permute-start | bytes 1769480 | tf_op jit(solution)/shard_map/ppermute | solution.py:806
  113.4 33.0 %collective-permute-start.24 = (bf16[4,96,768]{2,1,0:T(8,128)(2,1)}, bf16[4,96,768]{2,1,0:T(8,128)(2,1)}, u32[]{:S(2)}, u32[]{:S(2)}) collective-permute-start(bf16[4,96,768]{2,1,0:T(8,128)(2,1)} %collective-permute-done.16.down10_ref), channel_id=1, source_target_pairs={{0,1},{1,0},{2,3},{3,2},{4,5},{5,4},{6,7},{7,6},{8,9},{9,8},{10,11... | collective-permute-start | bytes 1769480 | tf_op jit(solution)/shard_map/ppermute | solution.py:806
  176.5 19.0 %collective-permute-start.28 = (bf16[512,768]{1,0:T(8,128)(2,1)}, bf16[512,768]{1,0:T(8,128)(2,1)}, u32[]{:S(2)}, u32[]{:S(2)}) collective-permute-start(bf16[512,768]{1,0:T(8,128)(2,1)} %get-tuple-element.291), channel_id=1, source_target_pairs={{0,8},{8,0},{16,24},{24,16},{1,9},{9,1},{17,25},{25,17},{2,10},{10... | collective-permute-start | bytes 2359304 | tf_op jit(solution)/shard_map/ppermute | solution.py:806
  176.6 41.3 %collective-permute-start.29 = (bf16[8,96,768]{2,1,0:T(8,128)(2,1)}, bf16[8,96,768]{2,1,0:T(8,128)(2,1)S(1)}, u32[]{:S(2)}, u32[]{:S(2)}) collective-permute-start(bf16[8,96,768]{2,1,0:T(8,128)(2,1)} %get-tuple-element.305), channel_id=1, source_target_pairs={{0,16},{8,24},{16,0},{24,8},{1,17},{9,25},{17,1},{25,9},{2,18},{10... | collective-permute-start | bytes 3538952 | tf_op jit(solution)/shard_map/ppermute | solution.py:806
  177.1 40.7 %collective-permute-start.30 = (bf16[4,2,96,768]{3,2,1,0:T(8,128)(2,1)}, bf16[4,2,96,768]{3,2,1,0:T(8,128)(2,1)}, u32[]{:S(2)}, u32[]{:S(2)}) collective-permute-start(bf16[4,2,96,768]{3,2,1,0:T(8,128)(2,1)} %get-tuple-element.306), channel_id=1, source_target_pairs={{0,1},{1,0},{2,3},{3,2},{4,5},{5,4},{6,7},{7,6},{8,9},{9,8},{10,11... | collective-permute-start | bytes 3538952 | tf_op jit(solution)/shard_map/ppermute | solution.py:806
  198.2 19.7 %collective-permute-start.31 = (bf16[256,768]{1,0:T(8,128)(2,1)S(1)}, bf16[256,768]{1,0:T(8,128)(2,1)S(1)}, u32[]{:S(2)}, u32[]{:S(2)}) collective-permute-start(bf16[256,768]{1,0:T(8,128)(2,1)S(1)} %copy-done.40), channel_id=1, source_target_pairs={{0,4},{1,5},{2,6},{3,7},{4,0},{5,1},{6,2},{7,3},{8,12},{9,13},{10,... | collective-permute-start | bytes 1179656 | tf_op jit(solution)/shard_map/ppermute | solution.py:806
  223.2 28.3 %collective-permute-start.34 = (bf16[256,768]{1,0:T(8,128)(2,1)}, bf16[256,768]{1,0:T(8,128)(2,1)}, u32[]{:S(2)}, u32[]{:S(2)}) collective-permute-start(bf16[256,768]{1,0:T(8,128)(2,1)} %pad_maximum_fusion.12), channel_id=1, source_target_pairs={{0,1},{1,0},{2,3},{3,2},{4,5},{5,4},{6,7},{7,6},{8,9},{9,8},{10,11... | collective-permute-start | bytes 1179656 | tf_op jit(solution)/shard_map/ppermute | solution.py:806
  224.7 26.8 %collective-permute-start.32 = (bf16[256,768]{1,0:T(8,128)(2,1)}, bf16[256,768]{1,0:T(8,128)(2,1)S(1)}, u32[]{:S(2)}, u32[]{:S(2)}) collective-permute-start(bf16[256,768]{1,0:T(8,128)(2,1)} %get-tuple-element.327.refs_20_), channel_id=1, source_target_pairs={{0,2},{1,3},{2,0},{3,1},{4,6},{5,7},{6,4},{7,5},{8,10},{9,11},{10,... | collective-permute-start | bytes 1179656 | tf_op jit(solution)/shard_map/ppermute | solution.py:806
  224.7 26.8 %collective-permute-start.33 = (bf16[256,768]{1,0:T(8,128)(2,1)}, bf16[256,768]{1,0:T(8,128)(2,1)S(1)}, u32[]{:S(2)}, u32[]{:S(2)}) collective-permute-start(bf16[256,768]{1,0:T(8,128)(2,1)} %get-tuple-element.328.refs_22_), channel_id=1, source_target_pairs={{0,6},{1,7},{2,4},{3,5},{4,2},{5,3},{6,0},{7,1},{8,14},{9,15},{10,... | collective-permute-start | bytes 1179656 | tf_op jit(solution)/shard_map/ppermute | solution.py:806
  226.3 25.2 %collective-permute-start.35 = (bf16[4,96,768]{2,1,0:T(8,128)(2,1)}, bf16[4,96,768]{2,1,0:T(8,128)(2,1)S(1)}, u32[]{:S(2)}, u32[]{:S(2)}) collective-permute-start(bf16[4,96,768]{2,1,0:T(8,128)(2,1)} %get-tuple-element.343), channel_id=1, source_target_pairs={{0,1},{1,0},{2,3},{3,2},{4,5},{5,4},{6,7},{7,6},{8,9},{9,8},{10,11... | collective-permute-start | bytes 1769480 | tf_op jit(solution)/shard_map/ppermute | solution.py:806
  226.9 24.7 %collective-permute-start.36 = (bf16[4,96,768]{2,1,0:T(8,128)(2,1)}, bf16[4,96,768]{2,1,0:T(8,128)(2,1)S(1)}, u32[]{:S(2)}, u32[]{:S(2)}) collective-permute-start(bf16[4,96,768]{2,1,0:T(8,128)(2,1)} %get-tuple-element.344), channel_id=1, source_target_pairs={{0,16},{8,24},{16,0},{24,8},{1,17},{9,25},{17,1},{25,9},{2,18},{10... | collective-permute-start | bytes 1769480 | tf_op jit(solution)/shard_map/ppermute | solution.py:806
  288.2 22.1 %collective-permute-start.49 = (bf16[256,768]{1,0:T(8,128)(2,1)}, bf16[256,768]{1,0:T(8,128)(2,1)S(1)}, u32[]{:S(2)}, u32[]{:S(2)}) collective-permute-start(bf16[256,768]{1,0:T(8,128)(2,1)} %get-tuple-element.399), channel_id=1, source_target_pairs={{0,1},{1,0},{2,3},{3,2},{4,5},{5,4},{6,7},{7,6},{8,9},{9,8},{10,11... | collective-permute-start | bytes 1179656 | tf_op jit(solution)/shard_map/ppermute | solution.py:806
  (72 other events, 568.1 us)
where the time goes:
time: 343 us; the launch traced here: 337 us
  Pallas kernels  139 us (41%)
  waiting for transfers between devices  104 us (30%)
  starting transfers between devices  49.2 us (14%)
  local copies, waits for them, and re-layouts  29.4 us (9%)
  other arithmetic  13.7 us (4%)
    ppermute x54, waiting for transfers between devices, over(): lax.ppermute(value, axis, [(i, i ^ bits) for i in range(lax.axis_size(axi...  104 us
    pallas_call x3, Pallas kernels, attn_bwd(): pl.pallas_call(lambda *refs: attn_bwd_kernel(units, *refs), grid=(3,), in...  50.2 us
    ppermute x54, starting transfers between devices, over(): lax.ppermute(value, axis, [(i, i ^ bits) for i in range(lax.axis_size(axi...  49.2 us
    pallas_call x1, Pallas kernels, attn_fwd(): pl.pallas_call(attn_fwd_kernel, grid=(3,), in_specs=[pl.BlockSpec(memory_...  31.4 us
    pallas_call x1, Pallas kernels, mlp(): pl.pallas_call(mlp_kernel, grid=(2,), in_specs=[pl.BlockSpec(memory_space...  24 us
    pallas_call x7, Pallas kernels, run_whole(): pl.pallas_call(kernel, in_specs=[pl.BlockSpec(memory_space=pltpu.SMEM)] +...  21.7 us
    unnamed x89, local copies, waits for them, and re-layouts  11.6 us
    pallas_call x1, Pallas kernels, branch(): pl.pallas_call(branch_kernel, grid=(1,), in_specs=[pl.BlockSpec((ROWS, D)...  7.01 us
  transfers between devices with their start and end apart: 54, of which 19 were waited for; matrix products, arithmetic and copies ran while one was open for 7% of the time, Pallas kernels for 30%

commit v1 on v0

--- a/solution.py
+++ b/solution.py
@@ -77,11 +77,16 @@
 
 
 def attn_fwd_kernel(
-    where_ref, x_ref, l00_ref, l10_ref, l01_ref, l11_ref, r00_ref, r10_ref, r01_ref, r11_ref,
-    w_ref, q_ref, k_ref, v_ref, e_ref, ec_ref, o_ref, r_ref, mid_ref, nm_ref, normed_ref,
-    bias_ref, att_ref, qs_ref, s_ref, inv_ref, out_ref, sems,
+    where_ref, x0_ref, x1_ref, x2_ref, x3_ref, xc_ref,
+    l00_ref, l10_ref, l01_ref, l11_ref, r00_ref, r10_ref, r01_ref, r11_ref,
+    w_out_ref, q_ref, k_ref, v_ref, e_ref, ec_ref, o_ref, r_ref, mid_ref, nm_ref, normed_out_ref,
+    w_ref, x_ref, normed_ref, bias_ref, att_ref, qs_ref, s_ref, inv_ref, out_ref, sems, out_sems,
 ):
     step = pl.program_id(0)
+    late = [
+        pltpu.make_async_copy(w_ref, w_out_ref, out_sems.at[0]),
+        pltpu.make_async_copy(normed_ref, normed_out_ref, out_sems.at[1]),
+    ]
 
     @pl.when(step == 0)
     def _():
@@ -120,6 +125,10 @@
                         sems.at[32 + at * 8 + i],
                     )
                 )
+        for at, part in enumerate((x0_ref, x1_ref, x2_ref, x3_ref, xc_ref)):
+            copies.append(
+                pltpu.make_async_copy(part, x_ref.at[pl.ds(at * UNIT, UNIT), :], sems.at[64 + at])
+            )
         for copy in copies:
             copy.start()
         pos = where_ref[0]
@@ -137,7 +146,9 @@
                     bias_ref[at] = jnp.full((PR, PR), jnp.where(seen, 0.0, neg_fill), F32)
         for copy in copies:
             copy.wait()
+        late[0].start()
         fill_normed(x_ref, gain_row(w_ref[0, :, HALF:]), normed_ref)
+        late[1].start()
 
     at = pl.ds(pl.multiple_of(step * UNIT, UNIT), UNIT)
     at_k = pl.ds(pl.multiple_of(D + step * UNIT, UNIT), UNIT)
@@ -211,9 +222,11 @@
                 middle = middle + dot_nn(att_ref[i, rows, :], wout[i * UNIT : (i + 1) * UNIT, :])
             mid_ref[rows, :] = middle
             nm_ref[rows, :] = (middle * rms_inv(middle) * gain).astype(BF)
-
-
-def attn_fwd(where, x_all, pieces):
+        for copy in late:
+            copy.wait()
+
+
+def attn_fwd(where, parts, pieces):
     pair = lambda i: (0, i)
     whole = lambda i: (0, 0)
     heads = lambda i: (i, 0, 0)
@@ -223,11 +236,10 @@
         grid=(3,),
         in_specs=[
             pl.BlockSpec(memory_space=pltpu.SMEM),
-            pl.BlockSpec((KEYS, D), whole),
-            *[anywhere] * 8,
+            *[anywhere] * 13,
         ],
         out_specs=[
-            pl.BlockSpec((2, D, WIDE), lambda i: (0, 0, 0)),
+            anywhere,
             pl.BlockSpec((ROWS, UNIT), pair),
             pl.BlockSpec((KEYS, UNIT), pair),
             pl.BlockSpec((KEYS, UNIT), pair),
@@ -237,7 +249,7 @@
             pl.BlockSpec((ROWS, UNIT), pair),
             pl.BlockSpec((ROWS, D), whole),
             pl.BlockSpec((ROWS, D), whole),
-            pl.BlockSpec((KEYS, D), whole),
+            anywhere,
         ],
         out_shape=[
             shape((2, D, WIDE), BF),
@@ -253,19 +265,23 @@
             shape((KEYS, D), BF),
         ],
         scratch_shapes=[
+            pltpu.VMEM((2, D, WIDE), BF),
+            pltpu.VMEM((KEYS, D), BF),
+            pltpu.VMEM((KEYS, D), BF),
             pltpu.VMEM((2 * PR, PLEN), F32),
             pltpu.VMEM((3, ROWS, UNIT), BF),
             pltpu.VMEM((2 * ROWS, WIDTH), BF),
             pltpu.VMEM((2 * ROWS, PLEN), F32),
             pltpu.VMEM((2 * ROWS, WIDTH), F32),
             pltpu.VMEM((2 * ROWS, WIDTH), F32),
-            pltpu.SemaphoreType.DMA((64,)),
+            pltpu.SemaphoreType.DMA((69,)),
+            pltpu.SemaphoreType.DMA((2,)),
         ],
         compiler_params=params(),
         cost_estimate=pl.CostEstimate(
             flops=30_000_000_000, bytes_accessed=30_000_000, transcendentals=6_300_000
         ),
-    )(where, x_all, *pieces)
+    )(where, *parts, *pieces)
 
 
 def mlp_kernel(
@@ -441,13 +457,15 @@
         dq_in_ref, *refs = refs
     wk_ref, wv_ref, *refs = refs
     if last:
-        where_ref, wq_ref, x_ref, normed_ref, kv1_ref, kv2_ref, kv3_ref, *refs = refs
+        where_ref, wq_ref, normed_ref, kv1_ref, kv2_ref, kv3_ref, *refs = refs
+        x_parts, refs = refs[:5], refs[5:]
         f1_ref, f2_ref, f3_ref, right_ref, *refs = refs
         keep_ref, give_ref, f0_ref, fc_ref, *refs = refs
-        late_in = (wq_ref, wk_ref, wv_ref, x_ref, normed_ref, right_ref)
+        late_in = (wq_ref, wk_ref, wv_ref, normed_ref, right_ref, *x_parts)
         *late, sems_late = refs[:7]
         refs = refs[7:]
-        wq_ref, wk_ref, wv_ref, x_ref, normed_ref, right_ref = late
+        wq_ref, wk_ref, wv_ref, normed_ref, right_ref, x_ref = late
+        late = late[:5] + [x_ref.at[pl.ds(at * UNIT, UNIT), :] for at in range(5)]
         dkv_ref, dq_ref, low_ref, high_ref, prod_ref, sems, *refs = refs
     else:
         dkv_refs, refs = refs[: len(units)], refs[len(units) :]
@@ -623,10 +641,10 @@
     args += [w_all, w_all]
     kv = (3, UNIT, 2 * UNIT)
     if last:
-        where, x_all, normed, kvs, fs, right = rest
-        specs += [pl.BlockSpec(memory_space=pltpu.SMEM)] + [anywhere] * 6
+        where, parts, normed, kvs, fs, right = rest
+        specs += [pl.BlockSpec(memory_space=pltpu.SMEM)] + [anywhere] * 10
         specs += [full(UNIT, D)] * 3 + [anywhere]
-        args += [where, w_all, x_all, normed, *kvs, *fs, right]
+        args += [where, w_all, normed, *kvs, *parts, *fs, right]
         outs = [anywhere, anywhere, full(UNIT, D), full(UNIT, D)]
         out_shapes = [shape((D, WIDE), BF)] * 2 + [shape((UNIT, D), F32)] * 2
         scratch = [
@@ -634,9 +652,9 @@
             pltpu.VMEM((1, D, D), BF),
             pltpu.VMEM((1, D, D), BF),
             pltpu.VMEM((KEYS, D), BF),
+            pltpu.VMEM((D, RIGHT), BF),
             pltpu.VMEM((KEYS, D), BF),
-            pltpu.VMEM((D, RIGHT), BF),
-            pltpu.SemaphoreType.DMA((6,)),
+            pltpu.SemaphoreType.DMA((10,)),
             pltpu.VMEM((3, KEYS, 2 * UNIT), BF),
             pltpu.VMEM((3, ROWS, UNIT), BF),
             pltpu.VMEM((D, WIDE), BF),
@@ -669,16 +687,17 @@
     )(*args)
 
 
-def tail_kernel(x_ref, f0_ref, f1_ref, f2_ref, f3_ref, fc_ref, dmid_ref, w_ref, keep_ref, give_ref):
+def tail_kernel(near_ref, cont_ref, f0_ref, f1_ref, f3_ref, fc_ref, dmid_ref, w_ref, keep_ref, give_ref):
     gain = gain_row(w_ref[0])
     for chunk in range(4):
         rows = slice(chunk * PR, (chunk + 1) * PR)
-        part = x_ref[rows, :].astype(F32)
+        at = slice(chunk % 2 * PR, (chunk % 2 + 1) * PR)
+        part = (near_ref if chunk < 2 else cont_ref)[at, :].astype(F32)
         inv = rms_inv(part)
         unit = part * inv
         if chunk < 2:
             grad = f0_ref[rows, :].astype(F32)
-            for f_ref in (f1_ref, f2_ref, f3_ref):
+            for f_ref in (f1_ref, f3_ref):
                 grad = grad + f_ref[rows, :].astype(F32)
         else:
             grad = fc_ref[(chunk - 2) * PR : (chunk - 1) * PR, :]
@@ -689,20 +708,20 @@
         out_ref[at, :] = (dmid_ref[rows, :] + inv * (scaled - unit * mean)).astype(out_ref.dtype)
 
 
-def tail(x_own, f_parts, f_cont, d_mid, w_all):
+def tail(near, cont, f_parts, f_cont, d_mid, w_all):
     whole = lambda i: (0, 0)
     half = pl.BlockSpec((2 * PR, D), whole)
     full = pl.BlockSpec((ROWS, D), whole)
     return pl.pallas_call(
         tail_kernel,
         grid=(1,),
-        in_specs=[full, half, half, half, half, half, full]
+        in_specs=[half, half, half, half, half, half, full]
         + [pl.BlockSpec((1, D, 128), lambda i: (0, 0, HALF // 128))],
         out_specs=[half, half],
         out_shape=[shape((2 * PR, D), F32), shape((2 * PR, D), BF)],
         compiler_params=params(),
         cost_estimate=pl.CostEstimate(flops=20_000_000, bytes_accessed=7_000_000, transcendentals=1000),
-    )(x_own, *f_parts, f_cont, d_mid, w_all)
+    )(near, cont, *f_parts, f_cont, d_mid, w_all)
 
 
 def total_of(*parts):
@@ -766,6 +785,24 @@
         for x in range(2):
             bk_ref[z, x] = block(2 * z + y_at, x, right)
             bg_ref[z, x] = block(2 * z + 1 - y_at, x, right)
+
+
+def split_cols_kernel(where_ref, a0_ref, a1_ref, a2_ref, a3_ref, left_ref, right_ref):
+    for at, ref in enumerate((a0_ref, a1_ref, a2_ref, a3_ref)):
+        left_ref[at] = ref[:, 0:LEFT]
+        right_ref[at] = ref[:, LEFT:]
+
+
+def join_kernel(where_ref, a0_ref, a1_ref, b0_ref, b1_ref, left_ref, right_ref):
+    for out_ref, parts in ((left_ref, (a0_ref, a1_ref)), (right_ref, (b0_ref, b1_ref))):
+        out_ref[0:4] = parts[0][...]
+        out_ref[4:8] = parts[1][...]
+
+
+def split_rows_kernel(where_ref, m0_ref, m1_ref, m2_ref, m3_ref, up_ref, down_ref):
+    for at, ref in enumerate((m0_ref, m1_ref, m2_ref, m3_ref)):
+        up_ref[at] = ref[0 : 2 * SUB, :]
+        down_ref[at] = ref[2 * SUB :, :]
 
 
 def unpack_kernel(where_ref, here_ref, far_ref, up_ref, down_ref):
@@ -788,8 +825,11 @@
                 )
 
 
-def finish_kernel(where_ref, own_ref, side_ref, core_ref, far_ref, qkv_ref, out_ref, gain_ref):
+def finish_kernel(
+    where_ref, own_ref, side_ref, core_ref, far_ref, qkv_ref, out_ref, gain_a_ref, gain_m_ref
+):
     first, near = where_ref[2] == 0, where_ref[1] == 0
+    columns = []
     for x in range(2):
         mine = jnp.where(near == (x == 0), own_ref[...], side_ref[...]).astype(F32)
         theirs = jnp.where(near == (x == 0), core_ref[...], far_ref[...]).astype(F32)
@@ -798,8 +838,10 @@
         qkv_ref[rows, 0:HALF] = low[:, 0:HALF]
         qkv_ref[rows, HALF:] = high[:, 0:D]
         out_ref[rows, :] = high[:, D:HALF]
-        gain_ref[rows, 0:128] = low[:, HALF:]
-        gain_ref[rows, 128:] = high[:, HALF:]
+        columns.append((low[:, HALF:], high[:, HALF:]))
+    for at, gain_ref in enumerate((gain_a_ref, gain_m_ref)):
+        both = jnp.concatenate([columns[0][at], columns[1][at]], axis=0)
+        gain_ref[...] = both.T[0:1, :]
 
 
 def over(axis, value, bits):
@@ -835,9 +877,11 @@
     def to_give(values):
         return jnp.concatenate([cut(values, (1 - y_at) * PR), cut(values, (3 - y_at) * PR)], axis=0)
 
-    def own_rows(values, got):
+    def own_parts(values, got):
         mine_p, mine_c = cut(values, y_at * PR), cut(values, (2 + y_at) * PR)
-        return jnp.concatenate([mine_p, got[:PR], mine_c, got[PR:]], axis=0)
+        return (
+            jnp.concatenate([mine_p, got[:PR]], axis=0), jnp.concatenate([mine_c, got[PR:]], axis=0)
+        )
 
     def to_return(values):
         return jnp.concatenate([values[PR : 2 * PR], values[3 * PR :]], axis=0)
@@ -879,35 +923,43 @@
             over("shard", to_give(tokens), 1),
             *[over("shard", own_piece, k) for k in (2, 4, 6)],
         )
-        x_own = own_rows(tokens, t_got)
-        near = x_own[: 2 * PR]
-        line = (own_piece, z1, z2, z3)
-        left = jnp.stack([part[:, :LEFT] for part in line])
-        right = jnp.stack([part[:, LEFT:] for part in line])
-        own_mlp, left, right, near = tie(own_mlp, left, right, near)
-        m1, m2, m3, left_y, right_x, g_got = tie(
-            *[over("shard", own_mlp, k) for k in (2, 4, 6)],
+        near, cont = own_parts(tokens, t_got)
+        left, right = run_whole(
+            split_cols_kernel, [(4, SUB, LEFT), (4, SUB, WIDE - LEFT)], where, own_piece, z1, z2, z3
+        )
+        own_mlp, near, left, right = tie(own_mlp, near, left, right)
+        m1, m3, left_y, right_x, g_got = tie(
+            over("shard", own_mlp, 2),
+            over("shard", own_mlp, 6),
             over("shard", left, 1),
             over("rep", right, 2),
             over("shard", to_give(d_out), 1),
         )
-        left = jnp.concatenate([left, left_y], axis=0)
-        right = jnp.concatenate([right, right_x], axis=0)
-        mlp_line = (own_mlp, m1, m2, m3)
-        up = jnp.stack([part[: 2 * SUB] for part in mlp_line])
-        down = jnp.stack([part[2 * SUB :] for part in mlp_line])
-        near, left, right, up, down = tie(near, left, right, up, down)
-        near1, near2, near3, left_x, right_y, up_y, down_x = tie(
-            *[over("shard", near, k) for k in (2, 4, 6)],
+        left, right = run_whole(
+            join_kernel, [(8, SUB, LEFT), (8, SUB, WIDE - LEFT)], where, left, left_y, right, right_x
+        )
+        m3, near, left, right = tie(m3, near, left, right)
+        m2, near3, left_x, right_y, left_core, right_core = tie(
+            over("shard", m3, 2),
+            over("shard", near, 6),
             over("rep", left, 2),
             over("shard", right, 1),
+            over("rep", left, 1),
+            over("rep", right, 1),
+        )
+        up, down = run_whole(
+            split_rows_kernel, [(4, 2 * SUB, D), (4, FSUB, D)], where, own_mlp, m1, m2, m3
+        )
+        near, near3, left_x, right_y, up, down = tie(near, near3, left_x, right_y, up, down)
+        near1, near2, up_y, down_x, left_far, right_far = tie(
+            over("shard", near, 2),
+            over("shard", near3, 2),
             over("shard", up, 1),
             over("rep", down, 2),
-        )
-        pieces = tie(
-            left, left_x, over("rep", left, 1), over("rep", left_x, 1),
-            right, right_y, over("rep", right, 1), over("rep", right_y, 1),
-        )
+            over("rep", left_x, 1),
+            over("rep", right_y, 1),
+        )
+        pieces = (left, left_x, left_core, left_far, right, right_y, right_core, right_far)
         up, up_y, down, down_x, pieces = tie(up, up_y, down, down_x, pieces)
         mlp_pieces = (
             up, over("rep", up, 2), up_y, over("rep", up_y, 2),
@@ -937,16 +989,15 @@
         mlp_pieces = tuple(
             pick_of(both[dy], side ^ dx, 1) for both in (up, down) for dy in (0, 1) for dx in (0, 1)
         )
-        x_own = own_rows(tokens, over("shard", to_give(tokens), 1))
-        near = x_own[: 2 * PR]
+        near, cont = own_parts(tokens, over("shard", to_give(tokens), 1))
         near1, near2, near3 = [over("shard", near, k) for k in (2, 4, 6)]
         g_got = over("shard", to_give(d_out), 1)
-    x_all = jnp.concatenate([near, near1, near2, near3, x_own[2 * PR :]], axis=0)
-    g_own = own_rows(d_out, g_got)
-    x_all, g_own = tie(x_all, g_own)
+    parts = (near, near1, near2, near3, cont)
+    g_own = jnp.concatenate(own_parts(d_out, g_got), axis=0)
+    parts, g_own = tie(parts, g_own)
 
     g_core = over("rep", g_own, 1)
-    forward = attn_fwd(where, x_all, pieces)
+    forward = attn_fwd(where, parts, pieces)
     forward, mlp_pieces, g_core = tie(forward, mlp_pieces, g_core)
     w_all, q, k, v, e, ec, attended, inv_sum, middle, nm, normed = forward
 
@@ -967,9 +1018,10 @@
     block_rows = (middle + y_own.astype(F32) + y_got.astype(F32)).astype(BF)
     block_give = to_return(block_rows)
     f2_give, dq, block_give = tie(f2_give, dq, block_give)
-    f2 = over("shard", f2_give, 4)
+    f2_got = over("shard", f2_give, 2)
     kv3, kv1, f3_give, f1_give, dq = attn_bwd((3, 1), saved, d_att, w_all, dq)
-    f2, f3_give, f1_give, dq, block_give = tie(f2, f3_give, f1_give, dq, block_give)
+    f2_got, f3_give, f1_give, dq, block_give = tie(f2_got, f3_give, f1_give, dq, block_give)
+    f3_send = total_of(f3_give, f2_got)
     if staged:
         up_got, down_got, dq = tie(up_got, down_got, dq)
         by_pair = (4, 2, 2 * SUB, D)
@@ -977,14 +1029,14 @@
             fold_two_kernel, [(4, 2 * SUB, D)] * 4, where,
             up_keep.reshape(by_pair), up_got.reshape(by_pair), down_keep, down_got,
         )
-        (up_keep, up_give, down_keep, down_give), dq, f3_give, f1_give, block_give = tie(
-            folded, dq, f3_give, f1_give, block_give
+        (up_keep, up_give, down_keep, down_give), dq, f3_send, f1_give, block_give = tie(
+            folded, dq, f3_send, f1_give, block_give
         )
         up_got, down_got = over("shard", up_give, 1), over("rep", down_give, 2)
-    f1, f3, b_got = over("shard", f1_give, 2), over("shard", f3_give, 6), over("shard", block_give, 1)
+    f1, f3, b_got = over("shard", f1_give, 2), over("shard", f3_send, 6), over("shard", block_give, 1)
     keep, give, f0, f_cont = attn_bwd(
         (0,), saved, d_att, w_all, dq,
-        (where, x_all, normed, (kv1, kv2, kv3), (f1_give, f2_give, f3_give), d_right),
+        (where, parts, normed, (kv1, kv2, kv3), (f1_give, f2_give, f3_give), d_right),
     )
     f1, f3, b_got, keep, give, f0, f_cont = tie(f1, f3, b_got, keep, give, f0, f_cont)
     if staged:
@@ -992,57 +1044,63 @@
         mlp_total, *mlp_gives = run_whole(
             fold_rows_kernel, [(4 * SUB, D)] * 4, where, up_keep, up_got, down_keep, down_got
         )
-        chip_got, mlp_gives = tie(over("rep", give, 1), mlp_gives)
+        chip_got, m2, mlp_gives = tie(
+            over("rep", give, 1), over("shard", mlp_gives[1], 2), mlp_gives
+        )
+        m1_send, m3_send = mlp_gives[0], total_of(mlp_gives[2], m2)
         left, right = (4, 2, SUB, LEFT), (4, 2, SUB, WIDE - LEFT)
         left_keep, left_give, right_keep, right_give = run_whole(
             fold_core_kernel, [left, left, right, right], where, keep, chip_got
         )
-        left_give, right_give, mlp_gives, f0 = tie(left_give, right_give, mlp_gives, f0)
-        left_got, right_got, m2, mlp_gives, token_keep, token_give = tie(
+        left_give, right_give, m1_send, m3_send, f0 = tie(
+            left_give, right_give, m1_send, m3_send, f0
+        )
+        left_got, right_got, m1, m3, token_keep, token_give = tie(
             over("rep", left_give, 2),
             over("shard", right_give, 1),
-            over("shard", mlp_gives[1], 4),
-            mlp_gives,
-            *tail(x_own, (f0, f1, f2, f3), f_cont, d_mid, w_all),
-        )
+            over("shard", m1_send, 2),
+            over("shard", m3_send, 6),
+            *tail(near, cont, (f0, f1, f3), f_cont, d_mid, w_all),
+        )
+        mlp_total = total_of(mlp_total, m1, m3)
         left_keep, left_give, right_keep, right_give = run_whole(
             fold_two_kernel,
             [(4, SUB, LEFT)] * 2 + [(4, SUB, WIDE - LEFT)] * 2,
             where, left_keep, left_got, right_keep, right_got,
         )
-        left_got, right_got, m1, m3 = tie(
+        left_got, right_got, m_got, mlp_total = tie(
             over("shard", left_give, 1),
             over("rep", right_give, 2),
-            over("shard", mlp_gives[0], 2),
-            over("shard", mlp_gives[2], 6),
+            over("rep", mlp_total, 2),
+            mlp_total,
         )
         total, *gives = run_whole(
             fold_cols_kernel, [(SUB, WIDE)] * 4, where, left_keep, left_got, right_keep, right_got
         )
-        gives, m1, m3 = tie(gives, m1, m3)
-        mlp_total = total_of(mlp_total, m1, m2, m3)
-        z1, z2, z3, m_got, mlp_total, t_got = tie(
+        by_side = jnp.stack([mlp_total, m_got])
+        gives, by_side = tie(gives, by_side)
+        z1, z2, z3, m_got, by_side, t_got = tie(
             *[over("shard", gives[step - 1], 2 * step) for step in (1, 2, 3)],
-            over("rep", mlp_total, 2),
-            mlp_total,
+            over("rep", by_side, 1),
+            by_side,
             over("shard", token_give, 1),
         )
         total = total_of(total, z1, z2, z3)
-        by_side = jnp.stack([mlp_total, m_got])
-        other, core_got, m_got, by_side = tie(
-            over("rep", total, 2), over("rep", total, 1), over("rep", by_side, 1), by_side
+        other, core_got, d_wup, d_wdown = tie(
+            over("rep", total, 2),
+            over("rep", total, 1),
+            *run_whole(
+                unpack_kernel, [(2 * SUB, FF), (4 * FSUB, D)], where, by_side, m_got, dtype=F32
+            ),
         )
         far = over("rep", other, 1)
-        d_wup, d_wdown = run_whole(
-            unpack_kernel, [(2 * SUB, FF), (4 * FSUB, D)], where, by_side, m_got, dtype=F32
-        )
-        d_wqkv, d_wout, d_gains = run_whole(
-            finish_kernel, [(2 * SUB, 3 * D), (2 * SUB, D), (2 * SUB, 256)],
+        d_wqkv, d_wout, d_gain_attn, d_gain_mlp = run_whole(
+            finish_kernel, [(2 * SUB, 3 * D), (2 * SUB, D), (1, 2 * SUB), (1, 2 * SUB)],
             where, total, other, core_got, far, dtype=F32,
         )
-        d_gain_attn, d_gain_mlp = d_gains[:, 0], d_gains[:, 128]
+        d_gain_attn, d_gain_mlp = d_gain_attn.reshape(2 * SUB), d_gain_mlp.reshape(2 * SUB)
     else:
-        token_keep, token_give = tail(x_own, (f0, f1, f2, f3), f_cont, d_mid, w_all)
+        token_keep, token_give = tail(near, cont, (f0, f1, f3), f_cont, d_mid, w_all)
         t_got = over("shard", token_give, 1)
         low, high = jnp.where(core == 0, keep, give), jnp.where(core == 0, give, keep)
 

time: 343 us -> 322 us (0.939)
  local copies, waits for them, and re-layouts: 29.4 us -> 13.2 us
  waiting for transfers between devices: 104 us -> 93.1 us
  starting transfers between devices: 49.2 us -> 56.6 us
  other arithmetic: 13.7 us -> 8.7 us
  Pallas kernels: 139 us -> 143 us
    ppermute x54, waiting for transfers between devices: 104 us -> 93.1 us  [over(): lax.ppermute(value, axis, [(i, i ^ bits) for i in range(lax.axis_size(axi...]
    ppermute x54, starting transfers between devices: 49.2 us -> 56.6 us  [over(): lax.ppermute(value, axis, [(i, i ^ bits) for i in range(lax.axis_size(axi...]
    pallas_call x7 -> x10, Pallas kernels: 21.7 us -> 28.6 us  [run_whole(): pl.pallas_call(kernel, in_specs=[pl.BlockSpec(memory_space=pltpu.SMEM)] +...]
    unnamed x89 -> x88, local copies, waits for them, and re-layouts: 11.6 us -> 6.04 us
    another operation x13 -> x1, local copies, waits for them, and re-layouts: 5.45 us -> 0.01 us  [the longest x4 2.69 us: per_device(): left = jnp.stack([part[:, :LEFT] for part in line])]
    slice x4 -> x2, local copies, waits for them, and re-layouts: 4.05 us -> 0.05 us  [the longest x1 0.03 us: own_parts(): got[PR:]]
  transfers between devices with their start and end apart: 54 -> 54, of which waited for: 19 -> 20; matrix products, arithmetic and copies ran while one was open for 7% -> 3% of each run, Pallas kernels for 30% -> 31%
where the time goes in v1:
time: 322 us; the launch traced here: 316 us
  Pallas kernels  143 us (44%)
  waiting for transfers between devices  93.1 us (29%)
  starting transfers between devices  56.6 us (18%)
  local copies, waits for them, and re-layouts  13.2 us (4%)
  other arithmetic  8.7 us (3%)
    ppermute x54, waiting for transfers between devices, over(): lax.ppermute(value, axis, [(i, i ^ bits) for i in range(lax.axis_size(axi...  93.1 us
    ppermute x54, starting transfers between devices, over(): lax.ppermute(value, axis, [(i, i ^ bits) for i in range(lax.axis_size(axi...  56.6 us
    pallas_call x3, Pallas kernels, attn_bwd(): pl.pallas_call(lambda *refs: attn_bwd_kernel(units, *refs), grid=(3,), in...  50.2 us
    pallas_call x1, Pallas kernels, attn_fwd(): pl.pallas_call(attn_fwd_kernel, grid=(3,), in_specs=[pl.BlockSpec(memory_...  29.1 us
    pallas_call x10, Pallas kernels, run_whole(): pl.pallas_call(kernel, in_specs=[pl.BlockSpec(memory_space=pltpu.SMEM)] +...  28.6 us
    pallas_call x1, Pallas kernels, mlp(): pl.pallas_call(mlp_kernel, grid=(2,), in_specs=[pl.BlockSpec(memory_space...  24 us
    pallas_call x1, Pallas kernels, branch(): pl.pallas_call(branch_kernel, grid=(1,), in_specs=[pl.BlockSpec((ROWS, D)...  7.02 us
  transfers between devices with their start and end apart: 54, of which 20 were waited for; matrix products, arithmetic and copies ran while one was open for 3% of the time, Pallas kernels for 31%

profile of v1, /device:TPU:0, one launch (start us, length us, event | category | flops | bytes accessed | tf_op | source)
XLA Modules:
  0.0 316.2 jit_solution(12600833950238883769)
XLA Ops:
  5.2 5.1 %collective-permute-start.3 = (bf16[48,1664]{1,0:T(8,128)(2,1)S(1)}, bf16[48,1664]{1,0:T(8,128)(2,1)}, u32[]{:S(2)}, u32[]{:S(2)}) collective-permute-start(bf16[48,1664]{1,0:T(8,128)(2,1)S(1)} %fusion.2.a0_ref), channel_id=1, source_target_pairs={{0,6},{1,7},{2,4},{3,5},{4,2},{5,3},{6,0},{7,1},{8,14},{9,15},{10,... | collective-permute-start | bytes 479240 | tf_op jit(solution)/shard_map/ppermute | solution.py:848
  16.9 7.1 %collective-permute-done.2.a2_ref = bf16[48,1664]{1,0:T(8,128)(2,1)} collective-permute-done((bf16[48,1664]{1,0:T(8,128)(2,1)S(1)}, bf16[48,1664]{1,0:T(8,128)(2,1)}, u32[]{:S(2)}, u32[]{:S(2)}) %collective-permute-start.2) | collective-permute-done | bytes 159776 | tf_op jit(solution)/shard_map/ppermute | solution.py:848
  32.2 3.5 %collective-permute-done.7.b1_ref = bf16[4,48,768]{2,1,0:T(8,128)(2,1)S(1)} collective-permute-done((bf16[4,48,768]{2,1,0:T(8,128)(2,1)}, bf16[4,48,768]{2,1,0:T(8,128)(2,1)S(1)}, u32[]{:S(2)}, u32[]{:S(2)}) %collective-permute-start.7) | collective-permute-done | bytes 294944 | tf_op jit(solution)/shard_map/ppermute | solution.py:848
  35.7 5.3 %collective-permute-done.5.m3_ref = bf16[192,768]{1,0:T(8,128)(2,1)S(1)} collective-permute-done((bf16[192,768]{1,0:T(8,128)(2,1)S(1)}, bf16[192,768]{1,0:T(8,128)(2,1)S(1)}, u32[]{:S(2)}, u32[]{:S(2)}) %collective-permute-start.5) | collective-permute-done | bytes 294944 | tf_op jit(solution)/shard_map/ppermute | solution.py:848
  41.0 3.9 %collective-permute-done.4.m1_ref = bf16[192,768]{1,0:T(8,128)(2,1)S(1)} collective-permute-done((bf16[192,768]{1,0:T(8,128)(2,1)S(1)}, bf16[192,768]{1,0:T(8,128)(2,1)S(1)}, u32[]{:S(2)}, u32[]{:S(2)}) %collective-permute-start.4) | collective-permute-done | bytes 294944 | tf_op jit(solution)/shard_map/ppermute | solution.py:848
  49.8 7.2 %collective-permute-done.9.m2_ref = bf16[192,768]{1,0:T(8,128)(2,1)S(1)} collective-permute-done((bf16[192,768]{1,0:T(8,128)(2,1)S(1)}, bf16[192,768]{1,0:T(8,128)(2,1)S(1)}, u32[]{:S(2)}, u32[]{:S(2)}) %collective-permute-start.9) | collective-permute-done | bytes 294944 | tf_op jit(solution)/shard_map/ppermute | solution.py:848
  58.0 11.2 %collective-permute-done.10.x3_ref.refs_22_ = bf16[256,768]{1,0:T(8,128)(2,1)S(1)} collective-permute-done((bf16[256,768]{1,0:T(8,128)(2,1)S(1)}, bf16[256,768]{1,0:T(8,128)(2,1)S(1)}, u32[]{:S(2)}, u32[]{:S(2)}) %collective-permute-start.10) | collective-permute-done | bytes 393248 | tf_op jit(solution)/shard_map/ppermute | solution.py:848
  71.7 6.6 %collective-permute-start.16 = (bf16[256,768]{1,0:T(8,128)(2,1)S(1)}, bf16[256,768]{1,0:T(8,128)(2,1)S(1)}, u32[]{:S(2)}, u32[]{:S(2)}) collective-permute-start(bf16[256,768]{1,0:T(8,128)(2,1)S(1)} %collective-permute-done.10.x3_ref.refs_22_), channel_id=1, source_target_pairs={{0,2},{1,3},{2,0},{3,1},{4,6},{5,7},{6,4},{7,5},{8,10},{9,11},{10,... | collective-permute-start | bytes 1179656 | tf_op jit(solution)/shard_map/ppermute | solution.py:848
  79.4 6.4 %collective-permute-done.16.x2_ref.refs_21_ = bf16[256,768]{1,0:T(8,128)(2,1)S(1)} collective-permute-done((bf16[256,768]{1,0:T(8,128)(2,1)S(1)}, bf16[256,768]{1,0:T(8,128)(2,1)S(1)}, u32[]{:S(2)}, u32[]{:S(2)}) %collective-permute-start.16) | collective-permute-done | bytes 393248 | tf_op jit(solution)/shard_map/ppermute | solution.py:848
  88.5 6.0 %collective-permute-done.15.x1_ref.refs_20_ = bf16[256,768]{1,0:T(8,128)(2,1)S(1)} collective-permute-done((bf16[256,768]{1,0:T(8,128)(2,1)S(1)}, bf16[256,768]{1,0:T(8,128)(2,1)S(1)}, u32[]{:S(2)}, u32[]{:S(2)}) %collective-permute-start.15) | collective-permute-done | bytes 393248 | tf_op jit(solution)/shard_map/ppermute | solution.py:848
  98.8 29.1 %shard_map.146 = (bf16[2,768,1664]{2,1,0:T(8,128)(2,1)}, bf16[512,768]{1,0:T(8,128)(2,1)}, bf16[1280,768]{1,0:T(8,128)(2,1)}, bf16[1280,768]{1,0:T(8,128)(2,1)},...) custom-call(s32[16]{0:T(128)} %stack.53.where_ref.refs_13_, ...), custom_call_target="tpu_custom_call" | custom-call | flops 30000001024 | bytes 30000000 | tf_op jit(solution)/shard_map/pallas_call | solution.py:234
  131.6 24.0 %shard_map.147 = (bf16[512,768]{1,0:T(8,128)(2,1)}, bf16[512,768]{1,0:T(8,128)(2,1)}, bf16[512,768]{1,0:T(8,128)(2,1)}, bf16[512,768]{1,0:T(8,128)(2,1)}, bf16[8...) custom-call(s32[16]{0:T(128)} %stack.53.where_ref.refs_13_, ...), custom_call_target="tpu_custom_call" | custom-call | flops 20000000000 | bytes 20000000 | tf_op jit(solution)/shard_map/pallas_call | solution.py:374
  160.5 7.0 %shard_map.148 = (f32[512,768]{1,0:T(8,128)}, bf16[512,768]{1,0:T(8,128)(2,1)}, bf16[768,896]{1,0:T(8,128)(2,1)}) custom-call(f32[512,768]{1,0:T(8,128)} %get-tuple-element.291.mid_ref, bf16[512,768]{1,0:T(8,128)(2,1)} %copy-done.3, bf16[512,768]{1,0:T(8,128)(2,1)} %get-tuple-element.313.e0_ref, bf16[512,768]{1,0:T(8,128)(2,1)} %copy-done.8, ...), custom_call_target="tpu_custom_call" | custom-call | flops 2000000000 | bytes 9000000 | tf_op jit(solution)/shard_map/pallas_call | solution.py:428
  167.6 10.8 %shard_map.149 = (bf16[3,256,512]{2,1,0:T(8,128)(2,1)}, bf16[256,768]{1,0:T(8,128)(2,1)}, f32[512,768]{1,0:T(8,128)}) custom-call(bf16[512,768]{1,0:T(8,128)(2,1)} %get-tuple-element.312.refs_0_, bf16[512,768]{1,0:T(8,128)(2,1)} %get-tuple-element.317.refs_1_, bf16[512,768]{1,0:T(8,128)(2,1)} %get-tuple-element.315.att_ref.refs_2_, ...), custom_call_target="tpu_custom_call" | custom-call | flops 10000000000 | bytes 10000000 | tf_op jit(solution)/shard_map/pallas_call | solution.py:670
  181.3 16.3 %shard_map.150 = (bf16[3,256,512]{2,1,0:T(8,128)(2,1)}, bf16[3,256,512]{2,1,0:T(8,128)(2,1)}, bf16[256,768]{1,0:T(8,128)(2,1)}, bf16[256,768]{1,0:T(8,128)(2,1)}, f32[512,768]{1,0:T(8,128)}) custom-call(bf16[512,768]{1,0:T(8,128)(2,1)} %get-tuple-element.312.refs_0_, bf16[512,768]{1,0:T(8,128)(2,1)} %get-tuple-element.317.refs_1_, ...), custom_call_target="tpu_custom_call" | custom-call | flops 20000000000 | bytes 10000000 | tf_op jit(solution)/shard_map/pallas_call | solution.py:670
  199.0 4.2 %shard_map.151 = (bf16[4,96,768]{2,1,0:T(8,128)(2,1)}, bf16[4,96,768]{2,1,0:T(8,128)(2,1)}, bf16[4,96,768]{2,1,0:T(8,128)(2,1)}, bf16[4,96,768]{2,1,0:T(8,128)(2,1)}) custom-call(s32[16]{0:T(128)} %stack.53.where_ref.refs_13_, bf16[4,2,96,768]{3,2,1,0:T(8,128)(2,1)} %bitcast.16, bf16[4,2,96,768]{3,2,1,0:T(8,128)(2,1)} %bitcast.17, ...), custom_call_target="tpu_custom_call" | custom-call | flops 1000000 | bytes 7000000 | tf_op jit(solution)/shard_map/pallas_call | solution.py:735
  208.7 23.1 %shard_map.152 = (bf16[768,1664]{1,0:T(8,128)(2,1)}, bf16[768,1664]{1,0:T(8,128)(2,1)}, f32[256,768]{1,0:T(8,128)}, f32[256,768]{1,0:T(8,128)}) custom-call(bf16[512,768]{1,0:T(8,128)(2,1)} %get-tuple-element.312.refs_0_, bf16[512,768]{1,0:T(8,128)(2,1)} %get-tuple-element.317.refs_1_, bf16[512,768]{1,0:T(8,128)(2,1)} %get-tuple-element.315.att_ref.refs_2_, ...), custom_call_target="tpu_custom_call" | custom-call | flops 20000000000 | bytes 10000000 | tf_op jit(solution)/shard_map/pallas_call | solution.py:670
  237.7 7.0 %collective-permute-done.38 = bf16[192,768]{1,0:T(8,128)(2,1)S(1)} collective-permute-done((bf16[192,768]{1,0:T(8,128)(2,1)}, bf16[192,768]{1,0:T(8,128)(2,1)S(1)}, u32[]{:S(2)}, u32[]{:S(2)}) %collective-permute-start.38) | collective-permute-done | bytes 294944 | tf_op jit(solution)/shard_map/ppermute | solution.py:848
  244.7 4.5 %shard_map.154 = (bf16[4,2,48,896]{3,2,1,0:T(8,128)(2,1)}, bf16[4,2,48,896]{3,2,1,0:T(8,128)(2,1)}, bf16[4,2,48,768]{3,2,1,0:T(8,128)(2,1)}, bf16[4,2,48,768]{3,2,1,0:T(8,128)(2,1)}) custom-call(s32[16]{0:T(128)} %stack.53.where_ref.refs_13_, bf16[768,1664]{1,0:T(8,128)(2,1)} %get-tuple-element.363.own_ref, bf16[768,1664]{1,0:T(8,128)(2,1)} %collective-permute-done.37.got_ref), custom_call_target="tpu_custom_call" | custom-call | flops 1000000 | bytes 7000000 | tf_op jit(solution)/shard_map/pallas_call | solution.py:735
  255.0 4.1 %shard_map.155 = (f32[256,768]{1,0:T(8,128)}, bf16[256,768]{1,0:T(8,128)(2,1)}) custom-call(bf16[256,768]{1,0:T(8,128)(2,1)} %copy-done.5, bf16[256,768]{1,0:T(8,128)(2,1)} %pad_maximum_fusion.7.xc_ref.refs_23_.cont_ref, f32[256,768]{1,0:T(8,128)} %get-tuple-element.386.f0_ref, bf16[256,768]{1,0:T(8,128)(2,1)} %copy-done.20, bf16[256,768]{1,0:T(8,128)(2,1)} %copy-done.19, ...), custom_call_target="tpu_custom_call" | custom-call | flops 20000000 | bytes 7000000 | tf_op jit(solution)/shard_map/pallas_call | solution.py:715
  260.9 5.6 %collective-permute-done.42 = bf16[192,768]{1,0:T(8,128)(2,1)S(1)} collective-permute-done((bf16[192,768]{1,0:T(8,128)(2,1)S(1)}, bf16[192,768]{1,0:T(8,128)(2,1)S(1)}, u32[]{:S(2)}, u32[]{:S(2)}) %collective-permute-start.42) | collective-permute-done | bytes 294944 | tf_op jit(solution)/shard_map/ppermute | solution.py:848
  273.3 6.6 %collective-permute-done.44.b1_ref = bf16[4,48,768]{2,1,0:T(8,128)(2,1)S(1)} collective-permute-done((bf16[4,48,768]{2,1,0:T(8,128)(2,1)}, bf16[4,48,768]{2,1,0:T(8,128)(2,1)S(1)}, u32[]{:S(2)}, u32[]{:S(2)}) %collective-permute-start.44) | collective-permute-done | bytes 294944 | tf_op jit(solution)/shard_map/ppermute | solution.py:848
  291.9 5.8 %collective-permute-done.50 = bf16[256,768]{1,0:T(8,128)(2,1)S(1)} collective-permute-done((bf16[256,768]{1,0:T(8,128)(2,1)}, bf16[256,768]{1,0:T(8,128)(2,1)S(1)}, u32[]{:S(2)}, u32[]{:S(2)}) %collective-permute-start.50) | collective-permute-done | bytes 393248 | tf_op jit(solution)/shard_map/ppermute | solution.py:848
  297.7 5.9 %collective-permute-done.47 = bf16[48,1664]{1,0:T(8,128)(2,1)S(1)} collective-permute-done((bf16[48,1664]{1,0:T(8,128)(2,1)}, bf16[48,1664]{1,0:T(8,128)(2,1)S(1)}, u32[]{:S(2)}, u32[]{:S(2)}) %collective-permute-start.47) | collective-permute-done | bytes 159776 | tf_op jit(solution)/shard_map/ppermute | solution.py:848
  (224 shorter events, 98.3 us)
Async XLA Ops:
  12.9 19.4 %collective-permute-start.8 = (bf16[256,768]{1,0:T(8,128)(2,1)S(1)}, bf16[256,768]{1,0:T(8,128)(2,1)S(1)}, u32[]{:S(2)}, u32[]{:S(2)}) collective-permute-start(bf16[256,768]{1,0:T(8,128)(2,1)S(1)} %pad_maximum_fusion.6), channel_id=1, source_target_pairs={{0,1},{1,0},{2,3},{3,2},{4,5},{5,4},{6,7},{7,6},{8,9},{9,8},{10,11... | collective-permute-start | bytes 1179656 | tf_op jit(solution)/shard_map/ppermute | solution.py:848
  26.2 18.7 %collective-permute-start.6 = (bf16[4,48,896]{2,1,0:T(8,128)(2,1)}, bf16[4,48,896]{2,1,0:T(8,128)(2,1)S(1)}, u32[]{:S(2)}, u32[]{:S(2)}) collective-permute-start(bf16[4,48,896]{2,1,0:T(8,128)(2,1)} %get-tuple-element.228.a0_ref), channel_id=1, source_target_pairs={{0,1},{1,0},{2,3},{3,2},{4,5},{5,4},{6,7},{7,6},{8,9},{9,8},{10,11... | collective-permute-start | bytes 1032200 | tf_op jit(solution)/shard_map/ppermute | solution.py:848
  48.6 20.7 %collective-permute-start.13 = (bf16[8,48,896]{2,1,0:T(8,128)(2,1)}, bf16[8,48,896]{2,1,0:T(8,128)(2,1)}, u32[]{:S(2)}, u32[]{:S(2)}) collective-permute-start(bf16[8,48,896]{2,1,0:T(8,128)(2,1)} %get-tuple-element.267.l00_ref), channel_id=1, source_target_pairs={{0,8},{8,0},{16,24},{24,16},{1,9},{9,1},{17,25},{25,17},{2,10},{10... | collective-permute-start | bytes 2064392 | tf_op jit(solution)/shard_map/ppermute | solution.py:848
  48.6 20.7 %collective-permute-start.11 = (bf16[8,48,896]{2,1,0:T(8,128)(2,1)}, bf16[8,48,896]{2,1,0:T(8,128)(2,1)}, u32[]{:S(2)}, u32[]{:S(2)}) collective-permute-start(bf16[8,48,896]{2,1,0:T(8,128)(2,1)} %get-tuple-element.267.l00_ref), channel_id=1, source_target_pairs={{0,16},{8,24},{16,0},{24,8},{1,17},{9,25},{17,1},{25,9},{2,18},{10... | collective-permute-start | bytes 2064392 | tf_op jit(solution)/shard_map/ppermute | solution.py:848
  49.1 20.2 %collective-permute-start.14 = (bf16[8,48,768]{2,1,0:T(8,128)(2,1)}, bf16[8,48,768]{2,1,0:T(8,128)(2,1)}, u32[]{:S(2)}, u32[]{:S(2)}) collective-permute-start(bf16[8,48,768]{2,1,0:T(8,128)(2,1)} %get-tuple-element.271.r00_ref), channel_id=1, source_target_pairs={{0,8},{8,0},{16,24},{24,16},{1,9},{9,1},{17,25},{25,17},{2,10},{10... | collective-permute-start | bytes 1769480 | tf_op jit(solution)/shard_map/ppermute | solution.py:848
  49.3 19.9 %collective-permute-start.12 = (bf16[8,48,768]{2,1,0:T(8,128)(2,1)}, bf16[8,48,768]{2,1,0:T(8,128)(2,1)}, u32[]{:S(2)}, u32[]{:S(2)}) collective-permute-start(bf16[8,48,768]{2,1,0:T(8,128)(2,1)} %get-tuple-element.271.r00_ref), channel_id=1, source_target_pairs={{0,1},{1,0},{2,3},{3,2},{4,5},{5,4},{6,7},{7,6},{8,9},{9,8},{10,11... | collective-permute-start | bytes 1769480 | tf_op jit(solution)/shard_map/ppermute | solution.py:848
  78.4 16.3 %collective-permute-start.19 = (bf16[8,48,896]{2,1,0:T(8,128)(2,1)}, bf16[8,48,896]{2,1,0:T(8,128)(2,1)S(1)}, u32[]{:S(2)}, u32[]{:S(2)}) collective-permute-start(bf16[8,48,896]{2,1,0:T(8,128)(2,1)} %collective-permute-done.11.l10_ref), channel_id=1, source_target_pairs={{0,8},{8,0},{16,24},{24,16},{1,9},{9,1},{17,25},{25,17},{2,10},{10... | collective-permute-start | bytes 2064392 | tf_op jit(solution)/shard_map/ppermute | solution.py:848
  94.7 33.2 %collective-permute-start.21 = (bf16[4,96,768]{2,1,0:T(8,128)(2,1)}, bf16[4,96,768]{2,1,0:T(8,128)(2,1)S(1)}, u32[]{:S(2)}, u32[]{:S(2)}) collective-permute-start(bf16[4,96,768]{2,1,0:T(8,128)(2,1)} %get-tuple-element.296.up00_ref), channel_id=1, source_target_pairs={{0,16},{8,24},{16,0},{24,8},{1,17},{9,25},{17,1},{25,9},{2,18},{10... | collective-permute-start | bytes 1769480 | tf_op jit(solution)/shard_map/ppermute | solution.py:848
  95.3 32.6 %collective-permute-start.22 = (bf16[4,96,768]{2,1,0:T(8,128)(2,1)}, bf16[4,96,768]{2,1,0:T(8,128)(2,1)S(1)}, u32[]{:S(2)}, u32[]{:S(2)}) collective-permute-start(bf16[4,96,768]{2,1,0:T(8,128)(2,1)} %collective-permute-done.17.up01_ref), channel_id=1, source_target_pairs={{0,16},{8,24},{16,0},{24,8},{1,17},{9,25},{17,1},{25,9},{2,18},{10... | collective-permute-start | bytes 1769480 | tf_op jit(solution)/shard_map/ppermute | solution.py:848
  96.8 31.2 %collective-permute-start.23 = (bf16[4,96,768]{2,1,0:T(8,128)(2,1)}, bf16[4,96,768]{2,1,0:T(8,128)(2,1)S(1)}, u32[]{:S(2)}, u32[]{:S(2)}) collective-permute-start(bf16[4,96,768]{2,1,0:T(8,128)(2,1)} %get-tuple-element.300.down00_ref), channel_id=1, source_target_pairs={{0,1},{1,0},{2,3},{3,2},{4,5},{5,4},{6,7},{7,6},{8,9},{9,8},{10,11... | collective-permute-start | bytes 1769480 | tf_op jit(solution)/shard_map/ppermute | solution.py:848
  98.3 29.7 %collective-permute-start.24 = (bf16[4,96,768]{2,1,0:T(8,128)(2,1)}, bf16[4,96,768]{2,1,0:T(8,128)(2,1)S(1)}, u32[]{:S(2)}, u32[]{:S(2)}) collective-permute-start(bf16[4,96,768]{2,1,0:T(8,128)(2,1)} %collective-permute-done.18.down10_ref), channel_id=1, source_target_pairs={{0,1},{1,0},{2,3},{3,2},{4,5},{5,4},{6,7},{7,6},{8,9},{9,8},{10,11... | collective-permute-start | bytes 1769480 | tf_op jit(solution)/shard_map/ppermute | solution.py:848
  98.8 29.2 %collective-permute-start.25 = (bf16[512,768]{1,0:T(8,128)(2,1)S(1)}, bf16[512,768]{1,0:T(8,128)(2,1)S(1)}, u32[]{:S(2)}, u32[]{:S(2)}) collective-permute-start(bf16[512,768]{1,0:T(8,128)(2,1)S(1)} %pad_maximum_fusion.1.g0_ref.g_ref), channel_id=1, source_target_pairs={{0,8},{8,0},{16,24},{24,16},{1,9},{9,1},{17,25},{25,17},{2,10},{10... | collective-permute-start | bytes 2359304 | tf_op jit(solution)/shard_map/ppermute | solution.py:848
  158.1 20.2 %collective-permute-start.28 = (bf16[512,768]{1,0:T(8,128)(2,1)}, bf16[512,768]{1,0:T(8,128)(2,1)}, u32[]{:S(2)}, u32[]{:S(2)}) collective-permute-start(bf16[512,768]{1,0:T(8,128)(2,1)} %get-tuple-element.311), channel_id=1, source_target_pairs={{0,8},{8,0},{16,24},{24,16},{1,9},{9,1},{17,25},{25,17},{2,10},{10... | collective-permute-start | bytes 2359304 | tf_op jit(solution)/shard_map/ppermute | solution.py:848
  158.5 39.1 %collective-permute-start.29 = (bf16[8,96,768]{2,1,0:T(8,128)(2,1)}, bf16[8,96,768]{2,1,0:T(8,128)(2,1)S(1)}, u32[]{:S(2)}, u32[]{:S(2)}) collective-permute-start(bf16[8,96,768]{2,1,0:T(8,128)(2,1)} %get-tuple-element.325), channel_id=1, source_target_pairs={{0,16},{8,24},{16,0},{24,8},{1,17},{9,25},{17,1},{25,9},{2,18},{10... | collective-permute-start | bytes 3538952 | tf_op jit(solution)/shard_map/ppermute | solution.py:848
  159.0 38.6 %collective-permute-start.30 = (bf16[4,2,96,768]{3,2,1,0:T(8,128)(2,1)}, bf16[4,2,96,768]{3,2,1,0:T(8,128)(2,1)}, u32[]{:S(2)}, u32[]{:S(2)}) collective-permute-start(bf16[4,2,96,768]{3,2,1,0:T(8,128)(2,1)} %get-tuple-element.326), channel_id=1, source_target_pairs={{0,1},{1,0},{2,3},{3,2},{4,5},{5,4},{6,7},{7,6},{8,9},{9,8},{10,11... | collective-permute-start | bytes 3538952 | tf_op jit(solution)/shard_map/ppermute | solution.py:848
  180.9 16.6 %collective-permute-start.31 = (bf16[256,768]{1,0:T(8,128)(2,1)S(1)}, bf16[256,768]{1,0:T(8,128)(2,1)S(1)}, u32[]{:S(2)}, u32[]{:S(2)}) collective-permute-start(bf16[256,768]{1,0:T(8,128)(2,1)S(1)} %copy-done.43), channel_id=1, source_target_pairs={{0,2},{1,3},{2,0},{3,1},{4,6},{5,7},{6,4},{7,5},{8,10},{9,11},{10,... | collective-permute-start | bytes 1179656 | tf_op jit(solution)/shard_map/ppermute | solution.py:848
  203.2 28.7 %collective-permute-start.33 = (bf16[256,768]{1,0:T(8,128)(2,1)S(1)}, bf16[256,768]{1,0:T(8,128)(2,1)S(1)}, u32[]{:S(2)}, u32[]{:S(2)}) collective-permute-start(bf16[256,768]{1,0:T(8,128)(2,1)S(1)} %add_convert_fusion.1), channel_id=1, source_target_pairs={{0,6},{1,7},{2,4},{3,5},{4,2},{5,3},{6,0},{7,1},{8,14},{9,15},{10,... | collective-permute-start | bytes 1179656 | tf_op jit(solution)/shard_map/ppermute | solution.py:848
  205.2 26.7 %collective-permute-start.34 = (bf16[256,768]{1,0:T(8,128)(2,1)S(1)}, bf16[256,768]{1,0:T(8,128)(2,1)S(1)}, u32[]{:S(2)}, u32[]{:S(2)}) collective-permute-start(bf16[256,768]{1,0:T(8,128)(2,1)S(1)} %pad_maximum_fusion.8), channel_id=1, source_target_pairs={{0,1},{1,0},{2,3},{3,2},{4,5},{5,4},{6,7},{7,6},{8,9},{9,8},{10,11... | collective-permute-start | bytes 1179656 | tf_op jit(solution)/shard_map/ppermute | solution.py:848
  206.7 25.2 %collective-permute-start.32 = (bf16[256,768]{1,0:T(8,128)(2,1)}, bf16[256,768]{1,0:T(8,128)(2,1)S(1)}, u32[]{:S(2)}, u32[]{:S(2)}) collective-permute-start(bf16[256,768]{1,0:T(8,128)(2,1)} %get-tuple-element.348.refs_24_), channel_id=1, source_target_pairs={{0,2},{1,3},{2,0},{3,1},{4,6},{5,7},{6,4},{7,5},{8,10},{9,11},{10,... | collective-permute-start | bytes 1179656 | tf_op jit(solution)/shard_map/ppermute | solution.py:848
  206.7 25.2 %collective-permute-start.35 = (bf16[4,96,768]{2,1,0:T(8,128)(2,1)}, bf16[4,96,768]{2,1,0:T(8,128)(2,1)S(1)}, u32[]{:S(2)}, u32[]{:S(2)}) collective-permute-start(bf16[4,96,768]{2,1,0:T(8,128)(2,1)} %get-tuple-element.364), channel_id=1, source_target_pairs={{0,1},{1,0},{2,3},{3,2},{4,5},{5,4},{6,7},{7,6},{8,9},{9,8},{10,11... | collective-permute-start | bytes 1769480 | tf_op jit(solution)/shard_map/ppermute | solution.py:848
  207.2 24.7 %collective-permute-start.36 = (bf16[4,96,768]{2,1,0:T(8,128)(2,1)}, bf16[4,96,768]{2,1,0:T(8,128)(2,1)S(1)}, u32[]{:S(2)}, u32[]{:S(2)}) collective-permute-start(bf16[4,96,768]{2,1,0:T(8,128)(2,1)} %get-tuple-element.365), channel_id=1, source_target_pairs={{0,16},{8,24},{16,0},{24,8},{1,17},{9,25},{17,1},{25,9},{2,18},{10... | collective-permute-start | bytes 1769480 | tf_op jit(solution)/shard_map/ppermute | solution.py:848
  249.3 17.2 %collective-permute-start.39 = (bf16[4,2,48,896]{3,2,1,0:T(8,128)(2,1)}, bf16[4,2,48,896]{3,2,1,0:T(8,128)(2,1)S(1)}, u32[]{:S(2)}, u32[]{:S(2)}) collective-permute-start(bf16[4,2,48,896]{3,2,1,0:T(8,128)(2,1)} %get-tuple-element.382), channel_id=1, source_target_pairs={{0,16},{8,24},{16,0},{24,8},{1,17},{9,25},{17,1},{25,9},{2,18},{10... | collective-permute-start | bytes 2064392 | tf_op jit(solution)/shard_map/ppermute | solution.py:848
  249.9 16.6 %collective-permute-start.40 = (bf16[4,2,48,768]{3,2,1,0:T(8,128)(2,1)}, bf16[4,2,48,768]{3,2,1,0:T(8,128)(2,1)S(1)}, u32[]{:S(2)}, u32[]{:S(2)}) collective-permute-start(bf16[4,2,48,768]{3,2,1,0:T(8,128)(2,1)} %get-tuple-element.383), channel_id=1, source_target_pairs={{0,1},{1,0},{2,3},{3,2},{4,5},{5,4},{6,7},{7,6},{8,9},{9,8},{10,11... | collective-permute-start | bytes 1769480 | tf_op jit(solution)/shard_map/ppermute | solution.py:848
  286.0 17.6 %collective-permute-start.49 = (bf16[2,192,768]{2,1,0:T(8,128)(2,1)S(1)}, bf16[2,192,768]{2,1,0:T(8,128)(2,1)S(1)}, u32[]{:S(2)}, u32[]{:S(2)}) collective-permute-start(bf16[2,192,768]{2,1,0:T(8,128)(2,1)S(1)} %pad_maximum_fusion.3.here_ref), channel_id=1, source_target_pairs={{0,8},{8,0},{16,24},{24,16},{1,9},{9,1},{17,25},{25,17},{2,10},{10... | collective-permute-start | bytes 1769480 | tf_op jit(solution)/shard_map/ppermute | solution.py:848
  (74 other events, 742.9 us)
